TPU v7x, 32 devices: a whole 2x2x4 slice. The times are simulated.
32 devices in a mesh: dp: 8 (over y, x, core), tensor: 4 (over z).
Axes of the slice: x: 2, y: 2, z: 4, core: 2. Of those that a mesh axis runs over, the one named last changes fastest.
Arguments:
- inputs: bfloat16 [4096, 5120], P(('dp', 'tensor')), may hold values from -6 to 6
- latent: bfloat16 [4096, 512], P(('dp', 'tensor')), may hold values from -180 to 180
- gain: float32 [512], replicated, may hold values from 0.25 to 1.75
- w_latent: bfloat16 [5120, 512], P('tensor'), may hold values from -0.078125 to 0.078125
- w_rope: bfloat16 [5120, 64], P('tensor'), may hold values from -0.078125 to 0.078125
- w_up: bfloat16 [512, 32768], P('dp', 'tensor'), may hold values from -0.25 to 0.25
- grad_kv: bfloat16 [4096, 32768], P('dp', 'tensor'), may hold values from -6 to 6
- grad_rope: bfloat16 [4096, 64], P(('dp', 'tensor')), may hold values from -6 to 6
Outputs:
- grad_x: bfloat16 [4096, 5120], P(('dp', 'tensor'))
- grad_w_up: bfloat16 [512, 32768], P('dp', 'tensor')
- grad_w_latent: bfloat16 [5120, 512], P('tensor', 'dp')
- grad_w_rope: bfloat16 [5120, 64], P('tensor', 'dp')
- grad_gain: float32 [512], replicated
All inputs are finite; a program needn't handle non-finite values.
Results may differ from a plain program's by a relative error of at most 0.019.
Values may be sent and summed in bfloat16 or wider, within the bound.
No kernel may reach another device: no remote copies, remote signals or barrier semaphores. Data moves between devices by JAX's collectives and lax.ppermute only.
A program may use at most 128 MiB of HBM per device.

v0:
```python
import jax
import jax.numpy as jnp
from jax import lax
from jax.sharding import PartitionSpec as P

epsilon = 1e-06


def contract(left, right, left_dim, right_dim):
    return lax.dot_general(
        left, right, (((left_dim,), (right_dim,)), ((), ())), preferred_element_type=jnp.float32
    )


def shards(inputs, latent, gain, w_latent, w_rope, w_up, grad_kv, grad_rope):
    latent_f = latent.astype(jnp.float32)
    inverse = lax.rsqrt(jnp.mean(latent_f * latent_f, axis=-1, keepdims=True) + epsilon)
    normed = (latent_f * inverse * gain).astype(jnp.bfloat16)
    up_full = lax.all_gather(w_up, "dp", axis=0, tiled=True)
    token_rows = grad_kv
    grad_norm = lax.psum_scatter(
        contract(token_rows, up_full, 1, 1), "tensor", scatter_dimension=0, tiled=True
    )
    token_rows = grad_kv
    up_partial = contract(lax.all_gather(normed, "tensor", axis=0, tiled=True), token_rows, 0, 0)
    grad_w_up = lax.psum_scatter(
        up_partial.astype(jnp.bfloat16), "dp", scatter_dimension=0, tiled=True
    )
    scaled = grad_norm * gain
    grad_pre = inverse * scaled - latent_f * inverse**3 * jnp.mean(
        scaled * latent_f, axis=-1, keepdims=True
    )
    grad_pre = grad_pre.astype(jnp.bfloat16)
    gain_part = jnp.sum(grad_norm * latent_f * inverse, axis=0)
    grad_gain = lax.psum(gain_part, ("dp", "tensor"))
    spread = lax.all_to_all(inputs, "tensor", split_axis=1, concat_axis=0, tiled=True)
    full_pre, full_rope = (
        lax.all_gather(grad_pre, "tensor", axis=0, tiled=True),
        lax.all_gather(grad_rope, "tensor", axis=0, tiled=True),
    )
    latent_part = contract(spread, full_pre, 0, 0)
    rope_part = contract(spread, full_rope, 0, 0)
    columns = (contract(full_pre, w_latent, 1, 1) + contract(full_rope, w_rope, 1, 1)).astype(
        jnp.bfloat16
    )
    grad_x = lax.all_to_all(columns, "tensor", split_axis=0, concat_axis=1, tiled=True)
    summed_latent, summed_rope = (
        lax.psum_scatter(latent_part, "dp", scatter_dimension=1, tiled=True),
        lax.psum_scatter(rope_part, "dp", scatter_dimension=1, tiled=True),
    )
    return (
        grad_x,
        grad_w_up,
        summed_latent.astype(jnp.bfloat16),
        summed_rope.astype(jnp.bfloat16),
        grad_gain,
    )


def solution(mesh):
    in_specs = (
        P(("dp", "tensor"), None),
        P(("dp", "tensor"), None),
        P(),
        P("tensor", None),
        P("tensor", None),
        P("dp", "tensor"),
        P("dp", "tensor"),
        P(("dp", "tensor"), None),
    )
    out_specs = (
        P(("dp", "tensor"), None),
        P("dp", "tensor"),
        P("tensor", "dp"),
        P("tensor", "dp"),
        P(),
    )
    return jax.shard_map(shards, mesh=mesh, in_specs=in_specs, out_specs=out_specs, check_vma=False)
```

profile of v0, /device:TPU:0, one launch (start us, length us, event | category | flops | bytes accessed | tf_op | source)
XLA Modules:
  0.0 271.5 jit_solution(3828065547843119189)
XLA Ops:
  7.2 0.7 all-gather.2.cloned.1.call-update
  7.9 2.4 copy.16
  10.3 6.3 %all-to-all-start.1 = ((bf16[128,4,1280]{0,2,1:T(8,128)(2,1)}), bf16[128,4,1280]{0,2,1:T(8,128)(2,1)S(1)}, u32[]{:S(2)}, u32[]{:S(2)}) async-start(bf16[128,4,1280]{0,2,1:T(8,128)(2,1)} %bitcast.24), calls=%async_computation.3 | async-start | bytes 2621440 | tf_op jit(solution)/shard_map/all_to_all | solution.py:36
  16.7 50.3 %all-gather.2.cloned.1.call-done = bf16[512,8192]{1,0:T(8,128)(2,1)} async-done(((bf16[64,8192]{1,0:T(8,128)(2,1)}), bf16[512,8192]{1,0:T(8,128)(2,1)}) %all-gather.2.cloned.1.call-update) | async-done | bytes 8388624 | tf_op jit(solution)/shard_map/all_gather | solution.py:19
  67.0 11.2 %fusion.10 = f32[512,512]{1,0:T(8,128)} fusion(bf16[512,8192]{1,0:T(8,128)(2,1)} %param.14, bf16[512,8192]{1,0:T(8,128)(2,1)} %all-gather.2.cloned.1.call-done), kind=kOutput, calls=%fused_computation.21 | convolution fusion | flops 4294967296 | bytes 17825792 | tf_op jit(solution)/shard_map/dot_general | solution.py:10
  78.4 12.5 %all_gather.14 = bf16[512,64]{0,1:T(8,128)(2,1)S(1)} all-gather(bf16[128,64]{0,1:T(8,128)(2,1)S(1)} %copy-done.4), channel_id=1, replica_groups=mesh['dp'=8,'tensor'=4] {'tensor'}, dimensions={0}, use_global_device_ids=true | all-gather | bytes 81920 | tf_op jit(solution)/shard_map/all_gather | solution.py:39
  91.0 1.0 copy-done.1
  92.1 1.6 copy.17
  93.7 1.1 fusion.12
  94.8 11.0 %reduce-scatter.5.cloned.1.call-done = f32[128,512]{1,0:T(8,128)} async-done(((f32[512,512]{1,0:T(8,128)}), f32[128,512]{1,0:T(8,128)}) %reduce-scatter.5.cloned.1.call-update) | async-done | bytes 262160 | tf_op jit(solution)/shard_map/reduce_scatter | solution.py:21
  105.8 1.1 fusion.9
  106.9 1.1 fusion.7
  108.0 16.3 %all_gather.13 = bf16[512,512]{1,0:T(8,128)(2,1)S(1)} all-gather(bf16[128,512]{1,0:T(8,128)(2,1)S(1)} %get-tuple-element.8), channel_id=1, replica_groups=mesh['dp'=8,'tensor'=4] {'tensor'}, dimensions={0}, use_global_device_ids=true | all-gather | bytes 655360 | tf_op jit(solution)/shard_map/all_gather | solution.py:38
  124.3 2.4 convolution_bitcast_fusion
  126.8 15.1 %all_gather.15 = bf16[512,512]{1,0:T(8,128)(2,1)S(1)} all-gather(bf16[128,512]{1,0:T(8,128)(2,1)S(1)} %get-tuple-element.7), channel_id=1, replica_groups=mesh['dp'=8,'tensor'=4] {'tensor'}, dimensions={0}, use_global_device_ids=true | all-gather | bytes 655360 | tf_op jit(solution)/shard_map/all_gather | solution.py:25
  141.9 10.1 %convolution_convert_fusion = bf16[512,8192]{1,0:T(8,128)(2,1)} fusion(bf16[512,512]{1,0:T(8,128)(2,1)S(1)} %all_gather.15, bf16[512,8192]{1,0:T(8,128)(2,1)} %param.14), kind=kOutput, calls=%fused_computation | convolution fusion | flops 4299161600 | bytes 17301504 | tf_op jit(solution)/shard_map/dot_general | solution.py:10
  152.1 0.9 fusion.11
  153.0 1.6 fusion
  154.6 3.6 %all-to-all-start = ((bf16[4,128,1280]{2,1,0:T(8,128)(2,1)}), bf16[4,128,1280]{2,1,0:T(8,128)(2,1)S(1)}, u32[]{:S(2)}, u32[]{:S(2)}) async-start(bf16[4,128,1280]{2,1,0:T(8,128)(2,1)} %bitcast.26), calls=%async_computation.1 | async-start | bytes 2621440 | tf_op jit(solution)/shard_map/all_to_all | solution.py:46
  158.2 1.4 convert_element_type.27
  159.6 43.9 %psum.7 = f32[512]{0:T(512)} all-reduce(f32[512]{0:T(512)S(1)} %get-tuple-element.5), channel_id=1, replica_groups=mesh['dp'=8,'tensor'=4] {'dp','tensor'}, use_global_device_ids=true, to_apply=%region_7.0 | all-reduce | flops 512 | bytes 4096 | tf_op jit(solution)/shard_map/psum | solution.py:35
  203.5 1.2 copy.18
  204.7 1.8 convert_element_type.26
  206.5 58.5 %reduce-scatter.7.cloned.1.call-done = bf16[64,8192]{1,0:T(8,128)(2,1)} async-done(((bf16[512,8192]{1,0:T(8,128)(2,1)}), bf16[64,8192]{1,0:T(8,128)(2,1)}) %reduce-scatter.7.cloned.1.call-update) | async-done | bytes 1048592 | tf_op jit(solution)/shard_map/reduce_scatter | solution.py:26
  (27 shorter events, 0.5 us)
Async XLA Ops:
  7.2 144.9 %copy-start = (bf16[1280,512]{1,0:T(8,128)(2,1)S(1)}, bf16[1280,512]{1,0:T(8,128)(2,1)}, u32[]{:S(2)}) copy-start(bf16[1280,512]{1,0:T(8,128)(2,1)} %param.11) | copy-start | bytes 3932164
  7.2 59.8 %all-gather.2.cloned.1.call-start = ((), (), s32[]{:S(2)}) async-start(), calls=%async_computation.6 | async-start | bytes 9437184 | tf_op jit(solution)/shard_map/all_gather | solution.py:19
  10.3 80.7 %all-to-all-start.1 = ((bf16[128,4,1280]{0,2,1:T(8,128)(2,1)}), bf16[128,4,1280]{0,2,1:T(8,128)(2,1)S(1)}, u32[]{:S(2)}, u32[]{:S(2)}) async-start(bf16[128,4,1280]{0,2,1:T(8,128)(2,1)} %bitcast.24), calls=%async_computation.3 | async-start | bytes 2621440 | tf_op jit(solution)/shard_map/all_to_all | solution.py:36
  16.7 61.7 %copy-start.4 = (bf16[128,64]{0,1:T(8,128)(2,1)S(1)}, bf16[128,64]{0,1:T(8,128)(2,1)}, u32[]{:S(2)}) copy-start(bf16[128,64]{0,1:T(8,128)(2,1)} %param.15) | copy-start | bytes 49156
  16.7 74.2 %copy-start.2 = (bf16[128,512]{1,0:T(8,128)(2,1)S(1)}, bf16[128,512]{1,0:T(8,128)(2,1)}, u32[]{:S(2)}) copy-start(bf16[128,512]{1,0:T(8,128)(2,1)} %param.9) | copy-start | bytes 393220
  16.7 89.2 %reduce-scatter.5.cloned.1.call-start = ((), (), s32[]{:S(2)}) async-start(), calls=%async_computation.7 | async-start | bytes 1310720 | tf_op jit(solution)/shard_map/reduce_scatter | solution.py:21
  78.3 27.5 %copy-start.5 = (f32[512]{0:T(512)S(1)}, f32[512]{0:T(512)}, u32[]{:S(2)}) copy-start(f32[512]{0:T(512)} %param.10) | copy-start | bytes 6148
  78.3 79.9 %reduce-scatter.11.cloned.1.call-start = ((), (), s32[]{:S(2)}) async-start(), calls=%async_computation.10 | async-start | bytes 368640 | tf_op jit(solution)/shard_map/reduce_scatter | solution.py:49
  91.0 1.1 copy-start.1
  94.8 109.9 %reduce-scatter.9.cloned.1.call-start = ((), (), s32[]{:S(2)}) async-start(), calls=%async_computation.9 | async-start | bytes 2949120 | tf_op jit(solution)/shard_map/reduce_scatter | solution.py:48
  126.8 138.2 %reduce-scatter.7.cloned.1.call-start = ((), (), s32[]{:S(2)}) async-start(), calls=%async_computation.8 | async-start | bytes 9437184 | tf_op jit(solution)/shard_map/reduce_scatter | solution.py:26
  152.0 0.9 copy-start.3
  154.6 48.9 %all-to-all-start = ((bf16[4,128,1280]{2,1,0:T(8,128)(2,1)}), bf16[4,128,1280]{2,1,0:T(8,128)(2,1)S(1)}, u32[]{:S(2)}, u32[]{:S(2)}) async-start(bf16[4,128,1280]{2,1,0:T(8,128)(2,1)} %bitcast.26), calls=%async_computation.1 | async-start | bytes 2621440 | tf_op jit(solution)/shard_map/all_to_all | solution.py:46
Sparse Core Ops, SparseCore 0:
  9.9 57.0 all-gather.1
  78.4 27.3 reduce-scatter.4
  109.2 32.6 reduce-scatter.10
  145.4 43.9 reduce-scatter.8
  193.6 71.2 reduce-scatter.6
where the time goes:
time: 272 us; the launch traced here: 271 us
  waiting for transfers between devices  121 us (44%)
  blocking collectives  87.8 us (32%)
  matrix products  27.3 us (10%)
  between operations  13.9 us (5%)
  starting transfers between devices  10.1 us (4%)
  local copies, waits for them, and re-layouts  6.34 us (2%)
  other arithmetic  5.49 us (2%)
    reduce_scatter x1, waiting for transfers between devices, shards(): lax.psum_scatter(up_partial.astype(jnp.bfloat16), 'dp', scatter_dimension...  58.5 us
    all_gather x1, waiting for transfers between devices, shards(): up_full = lax.all_gather(w_up, 'dp', axis=0, tiled=True)  50.3 us
    psum x1, blocking collectives, shards(): grad_gain = lax.psum(gain_part, ('dp', 'tensor'))  43.9 us
    dot_general x6, matrix products, contract(): lax.dot_general(left, right, (((left_dim,), (right_dim,)), ((), ())), pre...  27.3 us
    all_gather x1, blocking collectives, shards(): lax.all_gather(grad_pre, 'tensor', axis=0, tiled=True)  16.3 us
    all_gather x1, blocking collectives, shards(): lax.all_gather(normed, 'tensor', axis=0, tiled=True)  15.1 us
    all_gather x1, blocking collectives, shards(): lax.all_gather(grad_rope, 'tensor', axis=0, tiled=True)  12.5 us
    reduce_scatter x1, waiting for transfers between devices, shards(): lax.psum_scatter(contract(token_rows, up_full, 1, 1), 'tensor', scatter_d...  11 us
  transfers between devices with their start and end apart: 7, of which 3 were waited for; matrix products, arithmetic and copies ran while one was open for 14% of the time, Pallas kernels for 0%

commit v1 on v0

v1 whole, which is shorter than its diff:
```python
import functools

import jax
import jax.numpy as jnp
import numpy as np
from jax import lax
from jax.experimental import pallas as pl
from jax.experimental.pallas import tpu as pltpu
from jax.sharding import PartitionSpec as P

epsilon = 1e-06
W_U, W_M1, W_M2, W_COL, W_LAT = 2, 0, 16, 1, 8
LIMIT_U, LIMIT_M = 12, 12
F32 = jnp.float32
BF16 = jnp.bfloat16
VMEM = pl.BlockSpec(memory_space=pltpu.VMEM)
SMEM = pl.BlockSpec(memory_space=pltpu.SMEM)
GAIN_ROWS = 16


def dot(left, right, left_dim, right_dim):
    return lax.dot_general(
        left, right, (((left_dim,), (right_dim,)), ((), ())), preferred_element_type=F32
    )


def popcount(value):
    return bin(value).count("1")


def after(x, *done):
    return lax.optimization_barrier((x,) + done)[0]


def work(flops, moved, weight):
    return pl.CostEstimate(flops=weight * flops, bytes_accessed=weight * moved, transcendentals=0)


def call(body, name, out_shape, flops, weight, *args, scratch=(), limit=16):
    moved = sum(a.size * a.dtype.itemsize for a in args)
    return pl.pallas_call(
        body,
        in_specs=[SMEM] + [VMEM] * (len(args) - 1),
        out_specs=jax.tree.map(lambda _: VMEM, out_shape),
        out_shape=out_shape,
        scratch_shapes=scratch,
        compiler_params=pltpu.CompilerParams(vmem_limit_bytes=limit * 2**20),
        cost_estimate=work(flops, moved, weight),
        name=name,
    )(*args)


def split_rows(x, count, rows):
    at = lax.broadcasted_iota(jnp.int32, (rows, x.shape[1]), 0)
    result = jnp.zeros((rows, x.shape[1]), F32)
    for i in range(count):
        part = x.astype(BF16).astype(F32)
        result = jnp.where(at == i, part, result)
        x = x - part
    return result.astype(BF16)


class Plan:
    def __init__(self, groups, lanes, lat, rope):
        self.groups, self.lanes, self.lat, self.rope = groups, lanes, lat, rope
        self.axes = groups.bit_length() - 2
        self.slots = sorted(range(groups // 2), key=lambda slot: (popcount(slot), slot))
        middle = len(self.slots) // 2
        self.near, self.last = self.slots[:middle], self.slots[middle:]
        self.blk, self.rblk = lat // groups, rope // groups
        self.rb = max(self.rblk, 8)
        self.order = [(core, slot) for part in (self.near, self.last)
                      for core in (0, 1) for slot in part]

    def across(self, slot, core):
        bits = [self.axes - 1 - i if core else i for i in range(self.axes) if slot >> i & 1]
        return sum(2 << bit for bit in bits)

    def hop(self, slot):
        return 1 << (slot.bit_length() - 1)

    def rows_of(self, core):
        part = len(self.near) * self.blk
        first, second = core * part, (2 + core) * part
        return (first, first + part), (second, second + part)

    def pick_core(self, x, core):
        return jnp.concatenate([x[a:b] for a, b in self.rows_of(core)], axis=0)

    def place(self, me, order, block, stride):
        size, count = len(order) * stride, self.groups * block
        row = lax.broadcasted_iota(jnp.int32, (size, 1), 0)
        spot = jnp.full((size, 1), -1, jnp.int32)
        for b, (core, slot) in enumerate(order):
            rel = jnp.where(me % 2 == 0, self.across(slot, core) + core, self.across(slot, 1 - core) + core)
            start = (me ^ rel) * block
            inside = (row >= b * stride) & (row < b * stride + block)
            spot = jnp.where(inside, start + (row - b * stride), spot)
        column = lax.broadcasted_iota(jnp.int32, (size, count), 1)
        return (column == spot).astype(F32).astype(BF16)

    def place_latent(self, me):
        return self.place(me, self.order, self.blk, self.blk)

    def place_rope(self, me):
        order = [(core, slot) for core in (0, 1) for slot in self.slots]
        return self.place(me, order, self.rblk, self.rb)


def prep_kernel(plan, ids, gain, *refs):
    pieces, out_ref = refs[:-1], refs[-1]
    me, lane = ids[0], ids[1]
    tokens = pieces[0].shape[0]
    place = plan.place_latent(me)
    gain_col = jnp.sum(dot(place, split_rows(gain[...], 3, 8), 1, 1), axis=1, keepdims=True)
    for k, piece in enumerate(pieces):
        x = dot(place, piece[...], 1, 1)
        inverse = lax.rsqrt(jnp.sum(x * x, axis=0, keepdims=True) / plan.lat + epsilon)
        normed = (x * inverse * gain_col).astype(BF16)
        normed = jnp.concatenate([plan.pick_core(normed, 1), plan.pick_core(normed, 0)], axis=0)
        start = pl.multiple_of(lax.rem(lane - k + plan.lanes, plan.lanes) * tokens, tokens)
        out_ref[:, pl.ds(start, tokens)] = normed


def load_kernel(ids, x_ref, out_ref, sems):
    rows = x_ref.shape[0] // sems.shape[0]
    copies = [pltpu.make_async_copy(x_ref.at[pl.ds(i * rows, rows)], out_ref.at[pl.ds(i * rows, rows)],
                                    sems.at[i]) for i in range(sems.shape[0])]
    for copy in copies:
        copy.start()
    for copy in copies:
        copy.wait()


def load(ids, x):
    return pl.pallas_call(
        load_kernel,
        in_specs=[SMEM, pl.BlockSpec(memory_space=pltpu.HBM)],
        out_specs=VMEM,
        out_shape=pltpu.VMEM(x.shape, x.dtype),
        scratch_shapes=[pltpu.SemaphoreType.DMA((8,))],
        compiler_params=pltpu.CompilerParams(vmem_limit_bytes=2 * 2**20),
        cost_estimate=work(0, 0, 0),
        name="load",
    )(ids, x)


def up_kernel(ids, normed_ref, kv_ref, theirs_ref, *mine):
    half = theirs_ref.shape[0]
    rows = half // len(mine)
    depth = kv_ref.shape[1]
    step = min(depth, 1024)

    @pl.loop(0, depth // step)
    def _(k):
        at = pl.ds(pl.multiple_of(k * step, step), step)
        part = jnp.dot(normed_ref[...], kv_ref[:, at], preferred_element_type=F32)
        theirs_ref[:, at] = part[:half].astype(BF16)
        for i, out_ref in enumerate(mine):
            out_ref[:, at] = part[half + i * rows:half + (i + 1) * rows].astype(BF16)


def up_product(ids, normed_t, kv, count, weight):
    size, tokens = normed_t.shape
    depth = kv.shape[1]
    half = size // 2
    shapes = [half] + [half // count] * count
    return call(up_kernel, "up_product", [shape(rows, depth) for rows in shapes],
                2 * size * tokens * depth, weight, ids, normed_t, kv, limit=LIMIT_U)


def heads_kernel(count, lanes, ids, kv_ref, *refs):
    rows, before, outs, total = refs[:count], refs[count:-lanes - 1], refs[-lanes - 1:-1], refs[-1]
    depth = kv_ref.shape[1]
    step = min(depth, 1024)
    total[...] = jnp.zeros_like(total)

    @pl.loop(0, depth // step)
    def _(k):
        at = pl.ds(pl.multiple_of(k * step, step), step)
        total[...] += dot(kv_ref[:, at], jnp.concatenate([r[:, at] for r in rows], axis=0), 1, 1)

    tokens, columns = outs[0].shape[0], total.shape[1]
    for k, out_ref in enumerate(outs):
        start = pl.multiple_of(lax.rem(ids[1] + k, lanes) * tokens, tokens)
        if before:
            out_ref[:, :columns] = before[k][...]
        out_ref[:, out_ref.shape[1] - columns:] = total[pl.ds(start, tokens), :].astype(BF16)


def heads_product(ids, kv, rows, before, lanes, weight):
    tokens, depth = kv.shape
    width = sum(r.shape[0] for r in rows)
    out = shape(tokens // lanes, width + sum(b.shape[1] for b in before[:1]))
    return call(functools.partial(heads_kernel, len(rows), lanes), "heads_product", [out] * lanes,
                2 * tokens * depth * width, weight, ids, kv, *rows, *before,
                scratch=[pltpu.VMEM((tokens, width), F32)], limit=LIMIT_M)


def pre_kernel(plan, ids, latent, gain, rope_t, *refs):
    lanes = plan.lanes
    heads, out_ref = refs[:lanes], refs[lanes]
    tokens = latent.shape[0]
    place = plan.place_latent(ids[0])
    x = dot(latent[...], place, 1, 1)
    gain_row = jnp.sum(dot(split_rows(gain[...], 3, 8), place, 1, 1), axis=0, keepdims=True)
    grad_norm = sum(r[...].astype(F32) for r in heads)
    inverse = lax.rsqrt(jnp.sum(x * x, axis=1, keepdims=True) / plan.lat + epsilon)
    scaled = grad_norm * gain_row
    mean = jnp.sum(scaled * x, axis=1, keepdims=True) / plan.lat
    pre = inverse * scaled - x * (inverse * inverse * inverse) * mean
    out_ref[:tokens] = pre.astype(BF16)
    part = jnp.sum(grad_norm * x * inverse, axis=0, keepdims=True)
    part = jnp.sum(dot(split_rows(part, 3, 8), place, 1, 0), axis=0, keepdims=True)
    out_ref[tokens:tokens + GAIN_ROWS] = split_rows(part, 2, GAIN_ROWS)
    blocks = plan.lat // tokens
    rows = plan.rope // blocks
    out_ref[tokens + GAIN_ROWS:] = jnp.concatenate(
        [rope_t[i * rows:(i + 1) * rows, :] for i in range(blocks)], axis=1)


def rope_of(plan, message, tokens):
    blocks = plan.lat // tokens
    packed = message[tokens + GAIN_ROWS:]
    return jnp.concatenate(
        [packed[:, i * tokens:(i + 1) * tokens] for i in range(blocks)], axis=0)


def columns_kernel(plan, tokens, ids, *refs):
    lanes = plan.lanes
    messages, w_latent, w_rope_t, outs = refs[:lanes], refs[lanes], refs[lanes + 1], refs[lanes + 2:]
    pre = jnp.concatenate([m[:tokens] for m in messages], axis=0)
    pre = dot(pre, plan.place_latent(ids[0]), 1, 0).astype(BF16)
    rope = jnp.concatenate([rope_of(plan, m, tokens) for m in messages], axis=1)
    result = (dot(pre, w_latent[...], 1, 1) + dot(rope, w_rope_t[...], 0, 0)).astype(BF16)
    for k, out_ref in enumerate(outs):
        out_ref[...] = result[k * tokens:(k + 1) * tokens]


def gain_block(x, width):
    both = split_rows(x, 2, 8).astype(F32)
    row = jnp.concatenate([both[0:1], both[1:2]], axis=1)
    cut = row.shape[1]
    while cut > width:
        cut //= 2
    at = lax.broadcasted_iota(jnp.int32, (8, cut), 0)
    result = jnp.zeros((8, cut), F32)
    for i in range(row.shape[1] // cut):
        result = jnp.where(at == i, row[:, i * cut:(i + 1) * cut], result)
    if cut < width:
        result = jnp.concatenate([result, jnp.zeros((8, width - cut), F32)], axis=1)
    return result


def gain_of(block, lat):
    cut = 2 * lat
    while cut > block.shape[1]:
        cut //= 2
    row = jnp.concatenate([block[i:i + 1, :cut] for i in range(2 * lat // cut)], axis=1)
    return row[:, :lat] + row[:, lat:]


def latent_kernel(plan, tokens, ids, *refs):
    lanes = plan.lanes
    messages, spread, other_ref, own_ref = refs[:lanes], refs[lanes:2 * lanes], refs[-2], refs[-1]
    lane = ids[1]
    width = spread[0].shape[1]
    far = [lax.rem(lane - k + lanes, lanes) for k in range(lanes)]
    spread = jnp.concatenate([r[...] for r in spread], axis=0)
    pre = jnp.concatenate([m[:tokens] for m in messages], axis=0)
    rope_t = jnp.concatenate([rope_of(plan, m, tokens) for m in messages], axis=1)
    rope_t = dot(plan.place_rope(ids[0]), rope_t, 1, 0).astype(BF16)
    lat_rows = dot(pre, spread, 0, 0)
    rope_rows = dot(rope_t, spread, 1, 0)
    parts = [jnp.sum(m[tokens:tokens + GAIN_ROWS].astype(F32), axis=0, keepdims=True)
             for m in messages]
    total = jnp.zeros_like(parts[0])
    for j in range(lanes):
        term = parts[0]
        for k in range(1, lanes):
            term = jnp.where(far[j] == k, parts[k], term)
        total = total + term
    gain = gain_block(total, width)
    n = len(plan.slots) * plan.rb
    for core, ref in ((1, other_ref), (0, own_ref)):
        rows = jnp.concatenate(
            [plan.pick_core(lat_rows, core), rope_rows[core * n:(core + 1) * n],
             gain, jnp.zeros_like(gain)], axis=0)
        ref[...] = rows.astype(ref.dtype)


def chip_kernel(plan, ids, own, other, *outs):
    half, n = plan.lat // 2, len(plan.slots) * plan.rb
    width = own.shape[1]
    mine, came = own[...], other[...].astype(F32)
    total = mine + came
    gain = gain_of(mine[half + n:half + n + 8], plan.lat) + gain_of(came[half + n:half + n + 8], plan.lat)
    gain = gain_block(gain, width)
    for i, out_ref in enumerate(outs):
        rows = jnp.concatenate(
            [total[i * plan.blk:(i + 1) * plan.blk],
             total[half + i * plan.rb:half + (i + 1) * plan.rb], gain], axis=0)
        out_ref[...] = rows.astype(out_ref.dtype)


def last_kernel(plan, ids, *refs):
    count = len(plan.slots)
    back, sums = refs[:plan.lanes], refs[plan.lanes:plan.lanes + count]
    lat_ref, rope_ref, gain_ref, x_ref = refs[plan.lanes + count:]
    width = back[0].shape[1]
    for k, piece in enumerate(back):
        if width % 128 == 0:
            start = pl.multiple_of(lax.rem(ids[1] + k, plan.lanes) * width, width)
        else:
            start = k * width
        x_ref[:, pl.ds(start, width)] = piece[...]
    blk, rb = plan.blk, plan.rb
    me = ids[0]
    sums = [r[...].astype(F32) for r in sums]
    total = sum(s[:blk + rb] for s in sums)
    lat_ref[...] = total[:blk].astype(BF16)
    rope_ref[...] = total[blk:blk + rb].astype(BF16)
    parts = [gain_of(s[blk + rb:blk + rb + 8], plan.lat) for s in sums]
    gain = jnp.zeros_like(parts[0])
    for chip in range(plan.groups // 2):
        term = jnp.zeros_like(parts[0])
        for slot, part in zip(plan.slots, parts):
            rel = jnp.where(me % 2 == 0, plan.across(slot, 0) // 2, plan.across(slot, 1) // 2)
            term = jnp.where((rel ^ (me // 2)) == chip, part, term)
        gain = gain + term
    gain_ref[...] = gain


def cut_kernel(lanes, ids, x, *outs):
    width = outs[0].shape[1]
    for k, out_ref in enumerate(outs):
        start = pl.multiple_of(lax.rem(ids[1] + k, lanes) * width, width)
        out_ref[...] = x[:, pl.ds(start, width)]


def pick(pieces, index):
    result = pieces[0]
    for i in range(1, len(pieces)):
        result = jnp.where(index == i, pieces[i], result)
    return result


def add_kernel(*refs):
    refs[-1][...] = sum(r[...].astype(F32) for r in refs[:-1]).astype(BF16)


def add(*parts):
    parts = [p if isinstance(p, tuple) else (p, 0) for p in parts]
    rows, depth = parts[0][0].shape
    step = min(depth, 2048)
    return pl.pallas_call(
        add_kernel,
        grid=(depth // step,),
        in_specs=[pl.BlockSpec((rows, step), lambda k, at=at: (at // rows, k)) for _, at in parts],
        out_specs=pl.BlockSpec((rows, step), lambda k: (0, k)),
        out_shape=shape(rows, depth),
        compiler_params=pltpu.CompilerParams(vmem_limit_bytes=8 * 2**20),
        cost_estimate=work(0, 2 * rows * depth * (len(parts) + 1), 1),
        name="add",
    )(*[p for p, _ in parts])


def shape(rows, columns, dtype=BF16):
    return jax.ShapeDtypeStruct((rows, columns), dtype)


def make_shards(groups, lanes):
    def over_core(x):
        return lax.ppermute(x, "dp", [(i, i ^ 1) for i in range(groups)])

    def over_tensor(x, shift):
        return lax.ppermute(x, "tensor", [(i, (i + shift) % lanes) for i in range(lanes)])

    def shards(inputs, latent, gain, w_latent, w_rope, w_up, grad_kv, grad_rope):
        tokens, lat = latent.shape
        rope = grad_rope.shape[1]
        width = inputs.shape[1] // lanes
        plan = Plan(groups, lanes, lat, rope)
        slots, blk, rb = plan.slots, plan.blk, plan.rb
        me, lane = lax.axis_index("dp"), lax.axis_index("tensor")
        ids = jnp.stack([me, lane]).astype(jnp.int32)
        gain = gain[None, :]

        def over_plane(x, slot):
            return lax.ppermute(x, "dp", [(i, i ^ plan.across(slot, i % 2)) for i in range(groups)])

        held = {0: w_up}
        for slot in slots[1:]:
            if popcount(slot) == 1:
                held[slot] = over_plane(w_up if slot == 1 else after(w_up, held[1]), slot)
        if width % 128 == 0:
            cut = call(functools.partial(cut_kernel, lanes), "cut", [shape(tokens, width)] * lanes,
                       0, 0, ids, inputs)
        else:
            pieces = [inputs[:, j * width:(j + 1) * width] for j in range(lanes)]
            cut = [pick(pieces, lax.rem(lane + k, lanes)) for k in range(lanes)]
        spread = [cut[0]] + [over_tensor(cut[k], k) for k in range(1, lanes)]

        kv = load(ids, grad_kv)
        early = [latent] + [over_tensor(latent, k) for k in range(1, lanes)]
        normed_t = call(functools.partial(prep_kernel, plan), "prep", shape(lat, tokens * lanes),
                        0, 0, ids, gain, *early)

        for slot in slots[1:]:
            if popcount(slot) == 1:
                held[slot] = after(held[slot], kv, normed_t, cut[0])
        for slot in slots[1:]:
            if popcount(slot) > 1:
                held[slot] = over_plane(held[slot ^ plan.hop(slot)], plan.hop(slot))
        others = {slot: over_core(held[slot]) for slot in plan.near}

        def norm_part(part, weight, before, *done):
            rows = [(others if core else held)[slot] for core in (0, 1) for slot in part]
            rows[0] = after(rows[0], *done)
            return heads_product(ids, kv, rows, before, lanes, weight)

        near_heads = norm_part(plan.near, W_M1, [])
        theirs, *mine = up_product(ids, after(normed_t, near_heads[0]), kv, len(slots), W_U)
        came = over_core(theirs)
        for slot in plan.last:
            held[slot] = after(held[slot], theirs, *spread[1:])
            others[slot] = over_core(held[slot])
        heads = norm_part(plan.last, W_M2, near_heads)

        sums = {slot: [mine[i], (came, i * blk)] for i, slot in enumerate(slots)}
        far = [slot for slot in slots if popcount(slot) > 1]
        heads = [heads[0]] + [over_tensor(heads[k], k) for k in range(1, lanes)]

        for slot in reversed(far):
            sums[slot ^ plan.hop(slot)].append(over_plane(add(after(sums[slot][0], heads[0]), *sums[slot][1:]), plan.hop(slot)))

        going = {slot: add(*sums[slot]) for slot in slots if popcount(slot) == 1}
        lows = [over_plane(block, slot) for slot, block in going.items()]

        message = call(
            functools.partial(pre_kernel, plan), "pre",
            shape(tokens + GAIN_ROWS + rope * tokens // lat, lat),
            0, 0, ids, latent, gain, grad_rope.T, *heads)
        messages = [message] + [over_tensor(message, k) for k in range(1, lanes)]

        size = lat // 2 + len(slots) * rb + 16
        other, own = call(
            functools.partial(latent_kernel, plan, tokens), "latent_part",
            [shape(size, width), shape(size, width, F32)],
            2 * lat * tokens * lanes * width, W_LAT, ids, *messages,
            *spread[:-1], after(spread[-1], *going.values()))

        columns = call(
            functools.partial(columns_kernel, plan, tokens), "columns", [shape(tokens, width)] * lanes,
            2 * lat * tokens * lanes * (width + lat), W_COL, ids, *messages[:-1],
            after(messages[-1], other), w_latent, w_rope.T)
        back = [columns[0]] + [over_tensor(columns[k], -k) for k in range(1, lanes)]
        if width % 128 != 0:
            back = [pick(back, lax.rem(j + lanes - lane, lanes)) for j in range(lanes)]

        other = over_core(other)
        grad_w_up = add(*sums[0], *lows)
        size = blk + rb + 8
        blocks = call(
            functools.partial(chip_kernel, plan), "chip_sum",
            [shape(size, width, F32)] + [shape(size, width)] * (len(slots) - 1), 0, 0, ids,
            after(own, grad_w_up), other)
        blocks = [blocks[0]] + [over_plane(b, slot) for b, slot in zip(blocks[1:], slots[1:])]
        grad_lat, grad_rope, grad_gain, grad_x = call(
            functools.partial(last_kernel, plan), "last",
            [shape(blk, width), shape(rb, width), shape(1, lat, F32), shape(tokens, width * lanes)],
            0, 0, ids, *back, *blocks)
        return grad_x, grad_w_up, grad_lat.T, grad_rope[:plan.rblk].T, grad_gain[0]

    return shards


def solution(mesh):
    in_specs = (
        P(("dp", "tensor"), None),
        P(("dp", "tensor"), None),
        P(),
        P("tensor", None),
        P("tensor", None),
        P("dp", "tensor"),
        P("dp", "tensor"),
        P(("dp", "tensor"), None),
    )
    out_specs = (
        P(("dp", "tensor"), None),
        P("dp", "tensor"),
        P("tensor", "dp"),
        P("tensor", "dp"),
        P(),
    )
    shards = make_shards(mesh.shape["dp"], mesh.shape["tensor"])
    return jax.shard_map(shards, mesh=mesh, in_specs=in_specs, out_specs=out_specs, check_vma=False)
```

time: 272 us -> 134 us (0.49)
  blocking collectives: 87.8 us -> 0 us
  waiting for transfers between devices: 121 us -> 59.9 us
  Pallas kernels: 0 us -> 29.6 us
  starting transfers between devices: 10.1 us -> 39.1 us
  matrix products: 27.3 us -> 0 us
  between operations: 13.9 us -> 0.89 us
  other arithmetic: 5.49 us -> 0.07 us
    reduce_scatter x4 -> x0, waiting for transfers between devices: 69.5 us -> none  [the longest x1 58.5 us: shards(): lax.psum_scatter(up_partial.astype(jnp.bfloat16), 'dp', scatter_dimension...]
    ppermute x0 -> x30, waiting for transfers between devices: none -> 59.9 us  [the longest x15 48.1 us: over_tensor(): lax.ppermute(x, 'tensor', [(i, (i + shift) % lanes) for i in range(lanes)])]
    all_gather x1 -> x0, waiting for transfers between devices: 50.3 us -> none  [shards(): up_full = lax.all_gather(w_up, 'dp', axis=0, tiled=True)]
    psum x1 -> x0, blocking collectives: 43.9 us -> none  [shards(): grad_gain = lax.psum(gain_part, ('dp', 'tensor'))]
    all_gather x3 -> x0, blocking collectives: 43.8 us -> none  [the longest x1 16.3 us: shards(): lax.all_gather(grad_pre, 'tensor', axis=0, tiled=True)]
    ppermute x0 -> x30, starting transfers between devices: none -> 39.1 us  [the longest x15 27.1 us: over_tensor(): lax.ppermute(x, 'tensor', [(i, (i + shift) % lanes) for i in range(lanes)])]
    pallas_call x0 -> x15, Pallas kernels: none -> 29.6 us  [the longest x10 24.5 us: call(): pl.pallas_call(body, in_specs=[SMEM] + [VMEM] * (len(args) - 1), out_spec...]
    dot_general x6 -> x0, matrix products: 27.3 us -> none  [contract(): lax.dot_general(left, right, (((left_dim,), (right_dim,)), ((), ())), pre...]
  transfers between devices with their start and end apart: 7 -> 30, of which waited for: 3 -> 11; matrix products, arithmetic and copies ran while one was open for 14% -> 0% of each run, Pallas kernels for 0% -> 20%
where the time goes in v1:
time: 134 us
  waiting for transfers between devices  59.9 us (45%)
  starting transfers between devices  39.1 us (29%)
  Pallas kernels  29.6 us (22%)
  local copies, waits for them, and re-layouts  4.72 us (4%)
    ppermute x15, waiting for transfers between devices, over_tensor(): lax.ppermute(x, 'tensor', [(i, (i + shift) % lanes) for i in range(lanes)])  48.1 us
    ppermute x15, starting transfers between devices, over_tensor(): lax.ppermute(x, 'tensor', [(i, (i + shift) % lanes) for i in range(lanes)])  27.1 us
    pallas_call x10, Pallas kernels, call(): pl.pallas_call(body, in_specs=[SMEM] + [VMEM] * (len(args) - 1), out_spec...  24.5 us
    ppermute x9, starting transfers between devices, over_plane(): lax.ppermute(x, 'dp', [(i, i ^ plan.across(slot, i % 2)) for i in range(g...  11.4 us
    ppermute x9, waiting for transfers between devices, over_plane(): lax.ppermute(x, 'dp', [(i, i ^ plan.across(slot, i % 2)) for i in range(g...  6.69 us
    ppermute x6, waiting for transfers between devices, over_core(): return lax.ppermute(x, 'dp', [(i, i ^ 1) for i in range(groups)])  5.11 us
    unnamed x16, local copies, waits for them, and re-layouts  4.72 us
    pallas_call x4, Pallas kernels, add(): pl.pallas_call(add_kernel, grid=(depth // step,), in_specs=[pl.BlockSpec(...  3.84 us
  transfers between devices with their start and end apart: 30, of which 11 were waited for; matrix products, arithmetic and copies ran while one was open for 0% of the time, Pallas kernels for 20%

profile of v1, /device:TPU:0, one launch (start us, length us, event | category | flops | bytes accessed | tf_op | source)
XLA Modules:
  0.0 134.3 jit_solution(8796459585837995199)
XLA Ops:
  0.6 3.0 %collective-permute-start = (bf16[64,8192]{1,0:T(8,128)(2,1)}, bf16[64,8192]{1,0:T(8,128)(2,1)S(1)}, u32[]{:S(2)}, u32[]{:S(2)}) collective-permute-start(bf16[64,8192]{1,0:T(8,128)(2,1)} %refs_0_.2), channel_id=1, source_target_pairs={{0,8},{4,20},{8,0},{12,28},{16,24},{20,4},{24,16},{28,12},{1,9},{5... | collective-permute-start | bytes 3145736 | tf_op jit(solution)/shard_map/ppermute | solution.py:390
  3.6 3.6 %collective-permute-start.4 = (bf16[128,512]{1,0:T(8,128)(2,1)}, bf16[128,512]{1,0:T(8,128)(2,1)S(1)}, u32[]{:S(2)}, u32[]{:S(2)}) collective-permute-start(bf16[128,512]{1,0:T(8,128)(2,1)} %latent.1), channel_id=1, source_target_pairs={{0,3},{1,0},{2,1},{3,2},{4,7},{5,4},{6,5},{7,6},{8,11},{9,8},{10,9... | collective-permute-start | bytes 393224 | tf_op jit(solution)/shard_map/ppermute | solution.py:377
  10.3 3.4 %copy-done = bf16[512,8192]{1,0:T(8,128)(2,1)S(1)} copy-done((bf16[512,8192]{1,0:T(8,128)(2,1)S(1)}, bf16[512,8192]{1,0:T(8,128)(2,1)}, u32[]{:S(2)}) %copy-start) | copy-done | bytes 8388632
  14.9 3.4 %collective-permute-done.3.refs_2_ = bf16[128,512]{1,0:T(8,128)(2,1)S(1)} collective-permute-done((bf16[128,512]{1,0:T(8,128)(2,1)}, bf16[128,512]{1,0:T(8,128)(2,1)S(1)}, u32[]{:S(2)}, u32[]{:S(2)}) %collective-permute-start.3) | collective-permute-done | bytes 131104 | tf_op jit(solution)/shard_map/ppermute | solution.py:377
  22.9 1.8 %collective-permute-start.8 = (bf16[128,1280]{1,0:T(8,128)(2,1)S(1)}, bf16[128,1280]{1,0:T(8,128)(2,1)S(1)}, u32[]{:S(2)}, u32[]{:S(2)}) collective-permute-start(bf16[128,1280]{1,0:T(8,128)(2,1)S(1)} %get-tuple-element.54), channel_id=1, source_target_pairs={{0,2},{1,3},{2,0},{3,1},{4,6},{5,7},{6,4},{7,5},{8,10},{9,11},{10,... | collective-permute-start | bytes 983048 | tf_op jit(solution)/shard_map/ppermute | solution.py:377
  24.7 2.9 %collective-permute-start.9 = (bf16[128,1280]{1,0:T(8,128)(2,1)S(1)}, bf16[128,1280]{1,0:T(8,128)(2,1)S(1)}, u32[]{:S(2)}, u32[]{:S(2)}) collective-permute-start(bf16[128,1280]{1,0:T(8,128)(2,1)S(1)} %get-tuple-element.55), channel_id=1, source_target_pairs={{0,3},{1,0},{2,1},{3,2},{4,7},{5,4},{6,5},{7,6},{8,11},{9,8},{10,9... | collective-permute-start | bytes 983048 | tf_op jit(solution)/shard_map/ppermute | solution.py:377
  27.6 4.4 %heads_product.2 = (bf16[128,256]{1,0:T(8,128)(2,1)S(1)}, bf16[128,256]{1,0:T(8,128)(2,1)S(1)}, bf16[128,256]{1,0:T(8,128)(2,1)S(1)}, bf16[128,256]{1,0:T(8,128)(2,1)S(1)}) custom-call(s32[2]{0:T(128)S(1)} %pad_add_fusion.ids, bf16[512,8192]{1,0:T(8,128)(2,1)S(1)} %load.1.kv_ref, bf16[64,8192]{1,0:T(8,128)(2,1)S(1)} %copy-done.2, ...), custom_call_target="tpu_custom_call" | custom-call | tf_op jit(solution)/shard_map/heads_product/pallas_call | solution.py:41
  32.1 6.3 %up_product.1 = (bf16[256,8192]{1,0:T(8,128)(2,1)S(1)}, bf16[64,8192]{1,0:T(8,128)(2,1)S(1)}, bf16[64,8192]{1,0:T(8,128)(2,1)S(1)}, bf16[64,8192]{1,0:T(8,128)(2,1)S(1)}, bf16[64,8192]{1,0:T(8,128)(2,1)S(1)}) custom-call(s32[2]{0:T(128)S(1)} %pad_add_fusion.ids, bf16[512,512]{1,0:T(8,128)(2,1)S(1)} %prep.1.normed_ref, bf16[512,8192]{1,0:T(8,128)(2,1)S(1)} %load.1.kv_ref), custom_call_target="tpu_custom_call" | custom-call | flops 8589934592 | bytes 17825808 | tf_op jit(solution)/shard_map/up_product/pallas_call | solution.py:41
  38.4 9.3 %collective-permute-done.8.refs_6_ = bf16[128,1280]{1,0:T(8,128)(2,1)S(1)} collective-permute-done((bf16[128,1280]{1,0:T(8,128)(2,1)S(1)}, bf16[128,1280]{1,0:T(8,128)(2,1)S(1)}, u32[]{:S(2)}, u32[]{:S(2)}) %collective-permute-start.8) | collective-permute-done | bytes 327712 | tf_op jit(solution)/shard_map/ppermute | solution.py:377
  48.2 2.1 %collective-permute-done.11.refs_2_ = bf16[64,8192]{1,0:T(8,128)(2,1)S(1)} collective-permute-done((bf16[64,8192]{1,0:T(8,128)(2,1)S(1)}, bf16[64,8192]{1,0:T(8,128)(2,1)S(1)}, u32[]{:S(2)}, u32[]{:S(2)}) %collective-permute-start.11) | collective-permute-done | bytes 1048608 | tf_op jit(solution)/shard_map/ppermute | solution.py:374
  51.8 4.5 %heads_product.3 = (bf16[128,512]{1,0:T(8,128)(2,1)S(1)}, bf16[128,512]{1,0:T(8,128)(2,1)S(1)}, bf16[128,512]{1,0:T(8,128)(2,1)S(1)}, bf16[128,512]{1,0:T(8,128)(2,1)S(1)}) custom-call(s32[2]{0:T(128)S(1)} %pad_add_fusion.ids, bf16[512,8192]{1,0:T(8,128)(2,1)S(1)} %load.1.kv_ref, bf16[64,8192]{1,0:T(8,128)(2,1)S(1)} %collective-permute-done.1.refs_0_, ...), custom_call_target="tpu_custom_call" | custom-call | flops 34359738368 | bytes 205521024 | tf_op jit(solution)/shard_map/heads_product/pallas_call | solution.py:41
  59.7 6.6 %collective-permute-start.13 = (bf16[128,512]{1,0:T(8,128)(2,1)S(1)}, bf16[128,512]{1,0:T(8,128)(2,1)S(1)}, u32[]{:S(2)}, u32[]{:S(2)}) collective-permute-start(bf16[128,512]{1,0:T(8,128)(2,1)S(1)} %get-tuple-element.62), channel_id=1, source_target_pairs={{0,1},{1,2},{2,3},{3,0},{4,5},{5,6},{6,7},{7,4},{8,9},{9,10},{10,1... | collective-permute-start | bytes 393224 | tf_op jit(solution)/shard_map/ppermute | solution.py:377
  66.3 1.8 %collective-permute-start.14 = (bf16[128,512]{1,0:T(8,128)(2,1)S(1)}, bf16[128,512]{1,0:T(8,128)(2,1)S(1)}, u32[]{:S(2)}, u32[]{:S(2)}) collective-permute-start(bf16[128,512]{1,0:T(8,128)(2,1)S(1)} %get-tuple-element.63), channel_id=1, source_target_pairs={{0,2},{1,3},{2,0},{3,1},{4,6},{5,7},{6,4},{7,5},{8,10},{9,11},{10,... | collective-permute-start | bytes 393224 | tf_op jit(solution)/shard_map/ppermute | solution.py:377
  68.7 3.2 %collective-permute-done.13.refs_1_ = bf16[128,512]{1,0:T(8,128)(2,1)S(1)} collective-permute-done((bf16[128,512]{1,0:T(8,128)(2,1)S(1)}, bf16[128,512]{1,0:T(8,128)(2,1)S(1)}, u32[]{:S(2)}, u32[]{:S(2)}) %collective-permute-start.13) | collective-permute-done | bytes 131104 | tf_op jit(solution)/shard_map/ppermute | solution.py:377
  71.9 5.7 %collective-permute-done.14.refs_2_ = bf16[128,512]{1,0:T(8,128)(2,1)S(1)} collective-permute-done((bf16[128,512]{1,0:T(8,128)(2,1)S(1)}, bf16[128,512]{1,0:T(8,128)(2,1)S(1)}, u32[]{:S(2)}, u32[]{:S(2)}) %collective-permute-start.14) | collective-permute-done | bytes 131104 | tf_op jit(solution)/shard_map/ppermute | solution.py:377
  78.7 3.8 %collective-permute-start.18 = (bf16[160,512]{1,0:T(8,128)(2,1)S(1)}, bf16[160,512]{1,0:T(8,128)(2,1)S(1)}, u32[]{:S(2)}, u32[]{:S(2)}) collective-permute-start(bf16[160,512]{1,0:T(8,128)(2,1)S(1)} %pre.1.refs_0_), channel_id=1, source_target_pairs={{0,3},{1,0},{2,1},{3,2},{4,7},{5,4},{6,5},{7,6},{8,11},{9,8},{10,9... | collective-permute-start | bytes 491528 | tf_op jit(solution)/shard_map/ppermute | solution.py:377
  87.2 11.0 %collective-permute-done.17.refs_2_ = bf16[160,512]{1,0:T(8,128)(2,1)S(1)} collective-permute-done((bf16[160,512]{1,0:T(8,128)(2,1)S(1)}, bf16[160,512]{1,0:T(8,128)(2,1)S(1)}, u32[]{:S(2)}, u32[]{:S(2)}) %collective-permute-start.17) | collective-permute-done | bytes 163872 | tf_op jit(solution)/shard_map/ppermute | solution.py:377
  98.2 1.6 %latent_part.1 = (bf16[304,1280]{1,0:T(8,128)(2,1)S(1)}, f32[304,1280]{1,0:T(8,128)S(1)}) custom-call(s32[2]{0:T(128)S(1)} %pad_add_fusion.ids, bf16[160,512]{1,0:T(8,128)(2,1)S(1)} %pre.1.refs_0_, bf16[160,512]{1,0:T(8,128)(2,1)S(1)} %collective-permute-done.16.refs_1_, bf16[160,512]{1,0:T(8,128)(2,1)S(1)} %collective-permute-done.17.refs_2_, ...), custom_call_target="tpu_custom_call" | custom-call | flops 5368709120 | bytes 15728704 | tf_op jit(solution)/shard_map/latent_part/pallas_call | solution.py:41
  99.9 2.0 %columns.1 = (bf16[128,1280]{1,0:T(8,128)(2,1)S(1)}, bf16[128,1280]{1,0:T(8,128)(2,1)S(1)}, bf16[128,1280]{1,0:T(8,128)(2,1)S(1)}, bf16[128,1280]{1,0:T(8,128)(2,1)S(1)}) custom-call(s32[2]{0:T(128)S(1)} %pad_add_fusion.ids, bf16[160,512]{1,0:T(8,128)(2,1)S(1)} %pre.1.refs_0_, bf16[160,512]{1,0:T(8,128)(2,1)S(1)} %collective-permute-done.16.refs_1_, ...), custom_call_target="tpu_custom_call" | custom-call | flops 939524096 | bytes 2129928 | tf_op jit(solution)/shard_map/columns/pallas_call | solution.py:41
  103.2 6.7 %collective-permute-done.25.refs_3_ = bf16[64,8192]{1,0:T(8,128)(2,1)S(1)} collective-permute-done((bf16[64,8192]{1,0:T(8,128)(2,1)S(1)}, bf16[64,8192]{1,0:T(8,128)(2,1)S(1)}, u32[]{:S(2)}, u32[]{:S(2)}) %collective-permute-start.25) | collective-permute-done | bytes 1048608 | tf_op jit(solution)/shard_map/ppermute | solution.py:390
  109.8 1.8 %collective-permute-start.23 = (bf16[128,1280]{1,0:T(8,128)(2,1)S(1)}, bf16[128,1280]{1,0:T(8,128)(2,1)S(1)}, u32[]{:S(2)}, u32[]{:S(2)}) collective-permute-start(bf16[128,1280]{1,0:T(8,128)(2,1)S(1)} %get-tuple-element.75), channel_id=1, source_target_pairs={{0,1},{1,2},{2,3},{3,0},{4,5},{5,6},{6,7},{7,4},{8,9},{9,10},{10,1... | collective-permute-start | bytes 983048 | tf_op jit(solution)/shard_map/ppermute | solution.py:377
  111.7 2.1 %add.9 = bf16[64,8192]{1,0:T(8,128)(2,1)} custom-call(bf16[64,8192]{1,0:T(8,128)(2,1)S(1)} %get-tuple-element.77.refs_0_, bf16[256,8192]{1,0:T(8,128)(2,1)S(1)} %collective-permute-done.19.refs_1_, bf16[64,8192]{1,0:T(8,128)(2,1)S(1)} %collective-permute-done.24.refs_2_, bf16[64,8192]{1,0:T(8,128)(2,1)S(1)} %collective-permute-done.25.refs_3_), custom_call_target="tpu_custom_call" | custom-call | bytes 5242880 | tf_op jit(solution)/shard_map/add/pallas_call | solution.py:356
  118.0 14.5 %collective-permute-done.22.refs_2_ = bf16[128,1280]{1,0:T(8,128)(2,1)S(1)} collective-permute-done((bf16[128,1280]{1,0:T(8,128)(2,1)S(1)}, bf16[128,1280]{1,0:T(8,128)(2,1)S(1)}, u32[]{:S(2)}, u32[]{:S(2)}) %collective-permute-start.22) | collective-permute-done | bytes 327712 | tf_op jit(solution)/shard_map/ppermute | solution.py:377
  132.5 1.8 %last.1 = (bf16[64,1280]{1,0:T(8,128)(2,1)}, bf16[8,1280]{1,0:T(8,128)(2,1)}, f32[1,512]{1,0:T(1,128)}, bf16[128,5120]{1,0:T(8,128)(2,1)}) custom-call(s32[2]{0:T(128)S(1)} %pad_add_fusion.ids, bf16[128,1280]{1,0:T(8,128)(2,1)S(1)} %get-tuple-element.72.refs_0_, bf16[128,1280]{1,0:T(8,128)(2,1)S(1)} %collective-permute-done.21.refs_1_, ...), custom_call_target="tpu_custom_call" | custom-call | tf_op jit(solution)/shard_map/last/pallas_call | solution.py:41
  (68 shorter events, 26.2 us)
Async XLA Ops:
  0.6 19.2 %collective-permute-start = (bf16[64,8192]{1,0:T(8,128)(2,1)}, bf16[64,8192]{1,0:T(8,128)(2,1)S(1)}, u32[]{:S(2)}, u32[]{:S(2)}) collective-permute-start(bf16[64,8192]{1,0:T(8,128)(2,1)} %refs_0_.2), channel_id=1, source_target_pairs={{0,8},{4,20},{8,0},{12,28},{16,24},{20,4},{24,16},{28,12},{1,9},{5... | collective-permute-start | bytes 3145736 | tf_op jit(solution)/shard_map/ppermute | solution.py:390
  3.6 11.2 %collective-permute-start.4 = (bf16[128,512]{1,0:T(8,128)(2,1)}, bf16[128,512]{1,0:T(8,128)(2,1)S(1)}, u32[]{:S(2)}, u32[]{:S(2)}) collective-permute-start(bf16[128,512]{1,0:T(8,128)(2,1)} %latent.1), channel_id=1, source_target_pairs={{0,3},{1,0},{2,1},{3,2},{4,7},{5,4},{6,5},{7,6},{8,11},{9,8},{10,9... | collective-permute-start | bytes 393224 | tf_op jit(solution)/shard_map/ppermute | solution.py:377
  7.2 11.0 %collective-permute-start.3 = (bf16[128,512]{1,0:T(8,128)(2,1)}, bf16[128,512]{1,0:T(8,128)(2,1)S(1)}, u32[]{:S(2)}, u32[]{:S(2)}) collective-permute-start(bf16[128,512]{1,0:T(8,128)(2,1)} %latent.1), channel_id=1, source_target_pairs={{0,2},{1,3},{2,0},{3,1},{4,6},{5,7},{6,4},{7,5},{8,10},{9,11},{10,... | collective-permute-start | bytes 393224 | tf_op jit(solution)/shard_map/ppermute | solution.py:377
  7.2 11.0 %collective-permute-start.2 = (bf16[128,512]{1,0:T(8,128)(2,1)}, bf16[128,512]{1,0:T(8,128)(2,1)S(1)}, u32[]{:S(2)}, u32[]{:S(2)}) collective-permute-start(bf16[128,512]{1,0:T(8,128)(2,1)} %latent.1), channel_id=1, source_target_pairs={{0,1},{1,2},{2,3},{3,0},{4,5},{5,6},{6,7},{7,4},{8,9},{9,10},{10,1... | collective-permute-start | bytes 393224 | tf_op jit(solution)/shard_map/ppermute | solution.py:377
  8.3 14.7 %collective-permute-start.5 = (bf16[64,8192]{1,0:T(8,128)(2,1)}, bf16[64,8192]{1,0:T(8,128)(2,1)S(1)}, u32[]{:S(2)}, u32[]{:S(2)}) collective-permute-start(bf16[64,8192]{1,0:T(8,128)(2,1)} %refs_0_.2), channel_id=1, source_target_pairs={{0,4},{4,0},{8,12},{12,8},{16,20},{20,16},{24,28},{28,24},{1,5},{5... | collective-permute-start | bytes 3145736 | tf_op jit(solution)/shard_map/ppermute | solution.py:374
  19.9 18.5 %collective-permute-start.1 = (bf16[64,8192]{1,0:T(8,128)(2,1)S(1)}, bf16[64,8192]{1,0:T(8,128)(2,1)S(1)}, u32[]{:S(2)}, u32[]{:S(2)}) collective-permute-start(bf16[64,8192]{1,0:T(8,128)(2,1)S(1)} %copy-done.2), channel_id=1, source_target_pairs={{0,16},{4,12},{8,24},{12,4},{16,0},{20,28},{24,8},{28,20},{1,17},{... | collective-permute-start | bytes 3145736 | tf_op jit(solution)/shard_map/ppermute | solution.py:390
  21.4 26.2 %collective-permute-start.10 = (bf16[64,8192]{1,0:T(8,128)(2,1)S(1)}, bf16[64,8192]{1,0:T(8,128)(2,1)S(1)}, u32[]{:S(2)}, u32[]{:S(2)}) collective-permute-start(bf16[64,8192]{1,0:T(8,128)(2,1)S(1)} %collective-permute-done.refs_1_), channel_id=1, source_target_pairs={{0,16},{4,12},{8,24},{12,4},{16,0},{20,28},{24,8},{28,20},{1,17},{... | collective-permute-start | bytes 3145736 | tf_op jit(solution)/shard_map/ppermute | solution.py:390
  22.0 16.4 %collective-permute-start.7 = (bf16[128,1280]{1,0:T(8,128)(2,1)S(1)}, bf16[128,1280]{1,0:T(8,128)(2,1)S(1)}, u32[]{:S(2)}, u32[]{:S(2)}) collective-permute-start(bf16[128,1280]{1,0:T(8,128)(2,1)S(1)} %get-tuple-element.53), channel_id=1, source_target_pairs={{0,1},{1,2},{2,3},{3,0},{4,5},{5,6},{6,7},{7,4},{8,9},{9,10},{10,1... | collective-permute-start | bytes 983048 | tf_op jit(solution)/shard_map/ppermute | solution.py:377
  22.9 24.7 %collective-permute-start.8 = (bf16[128,1280]{1,0:T(8,128)(2,1)S(1)}, bf16[128,1280]{1,0:T(8,128)(2,1)S(1)}, u32[]{:S(2)}, u32[]{:S(2)}) collective-permute-start(bf16[128,1280]{1,0:T(8,128)(2,1)S(1)} %get-tuple-element.54), channel_id=1, source_target_pairs={{0,2},{1,3},{2,0},{3,1},{4,6},{5,7},{6,4},{7,5},{8,10},{9,11},{10,... | collective-permute-start | bytes 983048 | tf_op jit(solution)/shard_map/ppermute | solution.py:377
  24.7 22.9 %collective-permute-start.9 = (bf16[128,1280]{1,0:T(8,128)(2,1)S(1)}, bf16[128,1280]{1,0:T(8,128)(2,1)S(1)}, u32[]{:S(2)}, u32[]{:S(2)}) collective-permute-start(bf16[128,1280]{1,0:T(8,128)(2,1)S(1)} %get-tuple-element.55), channel_id=1, source_target_pairs={{0,3},{1,0},{2,1},{3,2},{4,7},{5,4},{6,5},{7,6},{8,11},{9,8},{10,9... | collective-permute-start | bytes 983048 | tf_op jit(solution)/shard_map/ppermute | solution.py:377
  58.4 26.4 %collective-permute-start.20 = (bf16[64,8192]{1,0:T(8,128)(2,1)S(1)}, bf16[64,8192]{1,0:T(8,128)(2,1)S(1)}, u32[]{:S(2)}, u32[]{:S(2)}) collective-permute-start(bf16[64,8192]{1,0:T(8,128)(2,1)S(1)} %add.6), channel_id=1, source_target_pairs={{0,16},{4,12},{8,24},{12,4},{16,0},{20,28},{24,8},{28,20},{1,17},{... | collective-permute-start | bytes 3145736 | tf_op jit(solution)/shard_map/ppermute | solution.py:390
  59.7 12.2 %collective-permute-start.13 = (bf16[128,512]{1,0:T(8,128)(2,1)S(1)}, bf16[128,512]{1,0:T(8,128)(2,1)S(1)}, u32[]{:S(2)}, u32[]{:S(2)}) collective-permute-start(bf16[128,512]{1,0:T(8,128)(2,1)S(1)} %get-tuple-element.62), channel_id=1, source_target_pairs={{0,1},{1,2},{2,3},{3,0},{4,5},{5,6},{6,7},{7,4},{8,9},{9,10},{10,1... | collective-permute-start | bytes 393224 | tf_op jit(solution)/shard_map/ppermute | solution.py:377
  66.3 11.2 %collective-permute-start.14 = (bf16[128,512]{1,0:T(8,128)(2,1)S(1)}, bf16[128,512]{1,0:T(8,128)(2,1)S(1)}, u32[]{:S(2)}, u32[]{:S(2)}) collective-permute-start(bf16[128,512]{1,0:T(8,128)(2,1)S(1)} %get-tuple-element.63), channel_id=1, source_target_pairs={{0,2},{1,3},{2,0},{3,1},{4,6},{5,7},{6,4},{7,5},{8,10},{9,11},{10,... | collective-permute-start | bytes 393224 | tf_op jit(solution)/shard_map/ppermute | solution.py:377
  82.5 15.7 %collective-permute-start.17 = (bf16[160,512]{1,0:T(8,128)(2,1)S(1)}, bf16[160,512]{1,0:T(8,128)(2,1)S(1)}, u32[]{:S(2)}, u32[]{:S(2)}) collective-permute-start(bf16[160,512]{1,0:T(8,128)(2,1)S(1)} %pre.1.refs_0_), channel_id=1, source_target_pairs={{0,2},{1,3},{2,0},{3,1},{4,6},{5,7},{6,4},{7,5},{8,10},{9,11},{10,... | collective-permute-start | bytes 491528 | tf_op jit(solution)/shard_map/ppermute | solution.py:377
  83.5 14.7 %collective-permute-start.16 = (bf16[160,512]{1,0:T(8,128)(2,1)S(1)}, bf16[160,512]{1,0:T(8,128)(2,1)S(1)}, u32[]{:S(2)}, u32[]{:S(2)}) collective-permute-start(bf16[160,512]{1,0:T(8,128)(2,1)S(1)} %pre.1.refs_0_), channel_id=1, source_target_pairs={{0,1},{1,2},{2,3},{3,0},{4,5},{5,6},{6,7},{7,4},{8,9},{9,10},{10,1... | collective-permute-start | bytes 491528 | tf_op jit(solution)/shard_map/ppermute | solution.py:377
  84.1 25.8 %collective-permute-start.25 = (bf16[64,8192]{1,0:T(8,128)(2,1)S(1)}, bf16[64,8192]{1,0:T(8,128)(2,1)S(1)}, u32[]{:S(2)}, u32[]{:S(2)}) collective-permute-start(bf16[64,8192]{1,0:T(8,128)(2,1)S(1)} %add.8), channel_id=1, source_target_pairs={{0,16},{4,12},{8,24},{12,4},{16,0},{20,28},{24,8},{28,20},{1,17},{... | collective-permute-start | bytes 3145736 | tf_op jit(solution)/shard_map/ppermute | solution.py:390
  85.5 26.2 %collective-permute-start.24 = (bf16[64,8192]{1,0:T(8,128)(2,1)S(1)}, bf16[64,8192]{1,0:T(8,128)(2,1)S(1)}, u32[]{:S(2)}, u32[]{:S(2)}) collective-permute-start(bf16[64,8192]{1,0:T(8,128)(2,1)S(1)} %add.7), channel_id=1, source_target_pairs={{0,8},{4,20},{8,0},{12,28},{16,24},{20,4},{24,16},{28,12},{1,9},{5... | collective-permute-start | bytes 3145736 | tf_op jit(solution)/shard_map/ppermute | solution.py:390
  99.8 13.9 %collective-permute-start.26 = (bf16[304,1280]{1,0:T(8,128)(2,1)S(1)}, bf16[304,1280]{1,0:T(8,128)(2,1)S(1)}, u32[]{:S(2)}, u32[]{:S(2)}) collective-permute-start(bf16[304,1280]{1,0:T(8,128)(2,1)S(1)} %get-tuple-element.70), channel_id=1, source_target_pairs={{0,4},{4,0},{8,12},{12,8},{16,20},{20,16},{24,28},{28,24},{1,5},{5... | collective-permute-start | bytes 2334728 | tf_op jit(solution)/shard_map/ppermute | solution.py:374
  102.0 14.5 %collective-permute-start.21 = (bf16[128,1280]{1,0:T(8,128)(2,1)S(1)}, bf16[128,1280]{1,0:T(8,128)(2,1)S(1)}, u32[]{:S(2)}, u32[]{:S(2)}) collective-permute-start(bf16[128,1280]{1,0:T(8,128)(2,1)S(1)} %get-tuple-element.73), channel_id=1, source_target_pairs={{0,3},{1,0},{2,1},{3,2},{4,7},{5,4},{6,5},{7,6},{8,11},{9,8},{10,9... | collective-permute-start | bytes 983048 | tf_op jit(solution)/shard_map/ppermute | solution.py:377
  102.0 30.5 %collective-permute-start.22 = (bf16[128,1280]{1,0:T(8,128)(2,1)S(1)}, bf16[128,1280]{1,0:T(8,128)(2,1)S(1)}, u32[]{:S(2)}, u32[]{:S(2)}) collective-permute-start(bf16[128,1280]{1,0:T(8,128)(2,1)S(1)} %get-tuple-element.74), channel_id=1, source_target_pairs={{0,2},{1,3},{2,0},{3,1},{4,6},{5,7},{6,4},{7,5},{8,10},{9,11},{10,... | collective-permute-start | bytes 983048 | tf_op jit(solution)/shard_map/ppermute | solution.py:377
  109.8 22.7 %collective-permute-start.23 = (bf16[128,1280]{1,0:T(8,128)(2,1)S(1)}, bf16[128,1280]{1,0:T(8,128)(2,1)S(1)}, u32[]{:S(2)}, u32[]{:S(2)}) collective-permute-start(bf16[128,1280]{1,0:T(8,128)(2,1)S(1)} %get-tuple-element.75), channel_id=1, source_target_pairs={{0,1},{1,2},{2,3},{3,0},{4,5},{5,6},{6,7},{7,4},{8,9},{9,10},{10,1... | collective-permute-start | bytes 983048 | tf_op jit(solution)/shard_map/ppermute | solution.py:377
  114.4 18.1 %collective-permute-start.27 = (bf16[80,1280]{1,0:T(8,128)(2,1)S(1)}, bf16[80,1280]{1,0:T(8,128)(2,1)S(1)}, u32[]{:S(2)}, u32[]{:S(2)}) collective-permute-start(bf16[80,1280]{1,0:T(8,128)(2,1)S(1)} %get-tuple-element.80), channel_id=1, source_target_pairs={{0,8},{4,20},{8,0},{12,28},{16,24},{20,4},{24,16},{28,12},{1,9},{5... | collective-permute-start | bytes 614408 | tf_op jit(solution)/shard_map/ppermute | solution.py:390
  115.7 16.8 %collective-permute-start.28 = (bf16[80,1280]{1,0:T(8,128)(2,1)S(1)}, bf16[80,1280]{1,0:T(8,128)(2,1)S(1)}, u32[]{:S(2)}, u32[]{:S(2)}) collective-permute-start(bf16[80,1280]{1,0:T(8,128)(2,1)S(1)} %get-tuple-element.81), channel_id=1, source_target_pairs={{0,16},{4,12},{8,24},{12,4},{16,0},{20,28},{24,8},{28,20},{1,17},{... | collective-permute-start | bytes 614408 | tf_op jit(solution)/shard_map/ppermute | solution.py:390
  116.5 16.0 %collective-permute-start.29 = (bf16[80,1280]{1,0:T(8,128)(2,1)S(1)}, bf16[80,1280]{1,0:T(8,128)(2,1)S(1)}, u32[]{:S(2)}, u32[]{:S(2)}) collective-permute-start(bf16[80,1280]{1,0:T(8,128)(2,1)S(1)} %get-tuple-element.82), channel_id=1, source_target_pairs={{0,24},{4,28},{8,16},{12,20},{16,8},{20,12},{24,0},{28,4},{1,25},{... | collective-permute-start | bytes 614408 | tf_op jit(solution)/shard_map/ppermute | solution.py:390
  (14 other events, 109.5 us)

commit v2 on v1

--- a/solution.py
+++ b/solution.py
@@ -408,7 +408,7 @@
 
         for slot in slots[1:]:
             if popcount(slot) == 1:
-                held[slot] = after(held[slot], kv, normed_t, cut[0])
+                held[slot] = after(held[slot], kv, cut[0], *early[1:])
         for slot in slots[1:]:
             if popcount(slot) > 1:
                 held[slot] = over_plane(held[slot ^ plan.hop(slot)], plan.hop(slot))
@@ -423,7 +423,7 @@
         theirs, *mine = up_product(ids, after(normed_t, near_heads[0]), kv, len(slots), W_U)
         came = over_core(theirs)
         for slot in plan.last:
-            held[slot] = after(held[slot], theirs, *spread[1:])
+            held[slot] = after(held[slot], theirs, spread[1], spread[-1])
             others[slot] = over_core(held[slot])
         heads = norm_part(plan.last, W_M2, near_heads)
 
@@ -432,7 +432,7 @@
         heads = [heads[0]] + [over_tensor(heads[k], k) for k in range(1, lanes)]
 
         for slot in reversed(far):
-            sums[slot ^ plan.hop(slot)].append(over_plane(add(after(sums[slot][0], heads[0]), *sums[slot][1:]), plan.hop(slot)))
+            sums[slot ^ plan.hop(slot)].append(over_plane(add(after(sums[slot][0], *heads[1:], *spread[2:-1]), *sums[slot][1:]), plan.hop(slot)))
 
         going = {slot: add(*sums[slot]) for slot in slots if popcount(slot) == 1}
         lows = [over_plane(block, slot) for slot, block in going.items()]
@@ -447,8 +447,7 @@
         other, own = call(
             functools.partial(latent_kernel, plan, tokens), "latent_part",
             [shape(size, width), shape(size, width, F32)],
-            2 * lat * tokens * lanes * width, W_LAT, ids, *messages,
-            *spread[:-1], after(spread[-1], *going.values()))
+            2 * lat * tokens * lanes * width, W_LAT, ids, *messages, *spread)
 
         columns = call(
             functools.partial(columns_kernel, plan, tokens), "columns", [shape(tokens, width)] * lanes,

time: 134 us -> 131 us (0.978)
  waiting for transfers between devices: 59.9 us -> 55.4 us
  starting transfers between devices: 39.1 us -> 40.6 us
    ppermute x15, waiting for transfers between devices: 48.1 us -> 36.5 us  [over_tensor(): lax.ppermute(x, 'tensor', [(i, (i + shift) % lanes) for i in range(lanes)])]
    ppermute x9, waiting for transfers between devices: 6.69 us -> 18 us  [over_plane(): lax.ppermute(x, 'dp', [(i, i ^ plan.across(slot, i % 2)) for i in range(g...]
    ppermute x6, waiting for transfers between devices: 5.11 us -> 0.91 us  [over_core(): return lax.ppermute(x, 'dp', [(i, i ^ 1) for i in range(groups)])]
  transfers between devices with their start and end apart: 30 -> 30, of which waited for: 11 -> 10; matrix products, arithmetic and copies ran while one was open for 0% -> 0% of each run, Pallas kernels for 20% -> 21%
where the time goes in v2:
time: 131 us
  waiting for transfers between devices  55.4 us (42%)
  starting transfers between devices  40.6 us (31%)
  Pallas kernels  29.5 us (23%)
  local copies, waits for them, and re-layouts  4.72 us (4%)
    ppermute x15, waiting for transfers between devices, over_tensor(): lax.ppermute(x, 'tensor', [(i, (i + shift) % lanes) for i in range(lanes)])  36.5 us
    ppermute x15, starting transfers between devices, over_tensor(): lax.ppermute(x, 'tensor', [(i, (i + shift) % lanes) for i in range(lanes)])  27.9 us
    pallas_call x10, Pallas kernels, call(): pl.pallas_call(body, in_specs=[SMEM] + [VMEM] * (len(args) - 1), out_spec...  24.5 us
    ppermute x9, waiting for transfers between devices, over_plane(): lax.ppermute(x, 'dp', [(i, i ^ plan.across(slot, i % 2)) for i in range(g...  18 us
    ppermute x9, starting transfers between devices, over_plane(): lax.ppermute(x, 'dp', [(i, i ^ plan.across(slot, i % 2)) for i in range(g...  12 us
    unnamed x16, local copies, waits for them, and re-layouts  4.72 us
    pallas_call x4, Pallas kernels, add(): pl.pallas_call(add_kernel, grid=(depth // step,), in_specs=[pl.BlockSpec(...  3.84 us
  transfers between devices with their start and end apart: 30, of which 10 were waited for; matrix products, arithmetic and copies ran while one was open for 0% of the time, Pallas kernels for 21%

profile of v2, /device:TPU:0, one launch (start us, length us, event | category | flops | bytes accessed | tf_op | source)
XLA Modules:
  0.0 131.2 jit_solution(5806215811305183898)
XLA Ops:
  0.6 3.0 %collective-permute-start = (bf16[64,8192]{1,0:T(8,128)(2,1)}, bf16[64,8192]{1,0:T(8,128)(2,1)S(1)}, u32[]{:S(2)}, u32[]{:S(2)}) collective-permute-start(bf16[64,8192]{1,0:T(8,128)(2,1)} %refs_0_.2), channel_id=1, source_target_pairs={{0,8},{4,20},{8,0},{12,28},{16,24},{20,4},{24,16},{28,12},{1,9},{5... | collective-permute-start | bytes 3145736 | tf_op jit(solution)/shard_map/ppermute | solution.py:390
  3.6 3.6 %collective-permute-start.4 = (bf16[128,512]{1,0:T(8,128)(2,1)}, bf16[128,512]{1,0:T(8,128)(2,1)S(1)}, u32[]{:S(2)}, u32[]{:S(2)}) collective-permute-start(bf16[128,512]{1,0:T(8,128)(2,1)} %latent.1), channel_id=1, source_target_pairs={{0,3},{1,0},{2,1},{3,2},{4,7},{5,4},{6,5},{7,6},{8,11},{9,8},{10,9... | collective-permute-start | bytes 393224 | tf_op jit(solution)/shard_map/ppermute | solution.py:377
  10.3 3.4 %copy-done = bf16[512,8192]{1,0:T(8,128)(2,1)S(1)} copy-done((bf16[512,8192]{1,0:T(8,128)(2,1)S(1)}, bf16[512,8192]{1,0:T(8,128)(2,1)}, u32[]{:S(2)}) %copy-start) | copy-done | bytes 8388632
  14.9 3.4 %collective-permute-done.3.refs_2_ = bf16[128,512]{1,0:T(8,128)(2,1)S(1)} collective-permute-done((bf16[128,512]{1,0:T(8,128)(2,1)}, bf16[128,512]{1,0:T(8,128)(2,1)S(1)}, u32[]{:S(2)}, u32[]{:S(2)}) %collective-permute-start.3) | collective-permute-done | bytes 131104 | tf_op jit(solution)/shard_map/ppermute | solution.py:377
  22.8 2.9 %collective-permute-start.8 = (bf16[128,1280]{1,0:T(8,128)(2,1)S(1)}, bf16[128,1280]{1,0:T(8,128)(2,1)S(1)}, u32[]{:S(2)}, u32[]{:S(2)}) collective-permute-start(bf16[128,1280]{1,0:T(8,128)(2,1)S(1)} %get-tuple-element.53), channel_id=1, source_target_pairs={{0,3},{1,0},{2,1},{3,2},{4,7},{5,4},{6,5},{7,6},{8,11},{9,8},{10,9... | collective-permute-start | bytes 983048 | tf_op jit(solution)/shard_map/ppermute | solution.py:377
  25.8 4.4 %heads_product.2 = (bf16[128,256]{1,0:T(8,128)(2,1)S(1)}, bf16[128,256]{1,0:T(8,128)(2,1)S(1)}, bf16[128,256]{1,0:T(8,128)(2,1)S(1)}, bf16[128,256]{1,0:T(8,128)(2,1)S(1)}) custom-call(s32[2]{0:T(128)S(1)} %pad_add_fusion.ids, bf16[512,8192]{1,0:T(8,128)(2,1)S(1)} %load.1.kv_ref, bf16[64,8192]{1,0:T(8,128)(2,1)S(1)} %copy-done.2, ...), custom_call_target="tpu_custom_call" | custom-call | tf_op jit(solution)/shard_map/heads_product/pallas_call | solution.py:41
  30.2 6.3 %up_product.1 = (bf16[256,8192]{1,0:T(8,128)(2,1)S(1)}, bf16[64,8192]{1,0:T(8,128)(2,1)S(1)}, bf16[64,8192]{1,0:T(8,128)(2,1)S(1)}, bf16[64,8192]{1,0:T(8,128)(2,1)S(1)}, bf16[64,8192]{1,0:T(8,128)(2,1)S(1)}) custom-call(s32[2]{0:T(128)S(1)} %pad_add_fusion.ids, bf16[512,512]{1,0:T(8,128)(2,1)S(1)} %prep.1.normed_ref, bf16[512,8192]{1,0:T(8,128)(2,1)S(1)} %load.1.kv_ref), custom_call_target="tpu_custom_call" | custom-call | flops 8589934592 | bytes 17825808 | tf_op jit(solution)/shard_map/up_product/pallas_call | solution.py:41
  36.5 2.4 %collective-permute-done.8.refs_7_ = bf16[128,1280]{1,0:T(8,128)(2,1)S(1)} collective-permute-done((bf16[128,1280]{1,0:T(8,128)(2,1)S(1)}, bf16[128,1280]{1,0:T(8,128)(2,1)S(1)}, u32[]{:S(2)}, u32[]{:S(2)}) %collective-permute-start.8) | collective-permute-done | bytes 327712 | tf_op jit(solution)/shard_map/ppermute | solution.py:377
  38.9 5.5 %collective-permute-done.9.refs_1_ = bf16[64,8192]{1,0:T(8,128)(2,1)S(1)} collective-permute-done((bf16[64,8192]{1,0:T(8,128)(2,1)S(1)}, bf16[64,8192]{1,0:T(8,128)(2,1)S(1)}, u32[]{:S(2)}, u32[]{:S(2)}) %collective-permute-start.9) | collective-permute-done | bytes 1048608 | tf_op jit(solution)/shard_map/ppermute | solution.py:390
  44.9 2.7 %collective-permute-start.18 = (bf16[128,1280]{1,0:T(8,128)(2,1)S(1)}, bf16[128,1280]{1,0:T(8,128)(2,1)S(1)}, u32[]{:S(2)}, u32[]{:S(2)}) collective-permute-start(bf16[128,1280]{1,0:T(8,128)(2,1)S(1)} %get-tuple-element.63), channel_id=1, source_target_pairs={{0,2},{1,3},{2,0},{3,1},{4,6},{5,7},{6,4},{7,5},{8,10},{9,11},{10,... | collective-permute-start | bytes 983048 | tf_op jit(solution)/shard_map/ppermute | solution.py:377
  48.6 4.4 %heads_product.3 = (bf16[128,512]{1,0:T(8,128)(2,1)S(1)}, bf16[128,512]{1,0:T(8,128)(2,1)S(1)}, bf16[128,512]{1,0:T(8,128)(2,1)S(1)}, bf16[128,512]{1,0:T(8,128)(2,1)S(1)}) custom-call(s32[2]{0:T(128)S(1)} %pad_add_fusion.ids, bf16[512,8192]{1,0:T(8,128)(2,1)S(1)} %load.1.kv_ref, bf16[64,8192]{1,0:T(8,128)(2,1)S(1)} %collective-permute-done.1.refs_0_, ...), custom_call_target="tpu_custom_call" | custom-call | flops 34359738368 | bytes 205521024 | tf_op jit(solution)/shard_map/heads_product/pallas_call | solution.py:41
  54.0 2.0 %collective-permute-start.13 = (bf16[128,512]{1,0:T(8,128)(2,1)S(1)}, bf16[128,512]{1,0:T(8,128)(2,1)S(1)}, u32[]{:S(2)}, u32[]{:S(2)}) collective-permute-start(bf16[128,512]{1,0:T(8,128)(2,1)S(1)} %get-tuple-element.61), channel_id=1, source_target_pairs={{0,2},{1,3},{2,0},{3,1},{4,6},{5,7},{6,4},{7,5},{8,10},{9,11},{10,... | collective-permute-start | bytes 393224 | tf_op jit(solution)/shard_map/ppermute | solution.py:377
  56.0 2.7 %collective-permute-start.14 = (bf16[128,512]{1,0:T(8,128)(2,1)S(1)}, bf16[128,512]{1,0:T(8,128)(2,1)S(1)}, u32[]{:S(2)}, u32[]{:S(2)}) collective-permute-start(bf16[128,512]{1,0:T(8,128)(2,1)S(1)} %get-tuple-element.62), channel_id=1, source_target_pairs={{0,3},{1,0},{2,1},{3,2},{4,7},{5,4},{6,5},{7,6},{8,11},{9,8},{10,9... | collective-permute-start | bytes 393224 | tf_op jit(solution)/shard_map/ppermute | solution.py:377
  58.7 10.2 %collective-permute-done.18.refs_6_ = bf16[128,1280]{1,0:T(8,128)(2,1)S(1)} collective-permute-done((bf16[128,1280]{1,0:T(8,128)(2,1)S(1)}, bf16[128,1280]{1,0:T(8,128)(2,1)S(1)}, u32[]{:S(2)}, u32[]{:S(2)}) %collective-permute-start.18) | collective-permute-done | bytes 327712 | tf_op jit(solution)/shard_map/ppermute | solution.py:377
  68.9 2.8 %collective-permute-done.13.refs_2_ = bf16[128,512]{1,0:T(8,128)(2,1)S(1)} collective-permute-done((bf16[128,512]{1,0:T(8,128)(2,1)S(1)}, bf16[128,512]{1,0:T(8,128)(2,1)S(1)}, u32[]{:S(2)}, u32[]{:S(2)}) %collective-permute-start.13) | collective-permute-done | bytes 131104 | tf_op jit(solution)/shard_map/ppermute | solution.py:377
  74.5 5.5 %collective-permute-start.17 = (bf16[160,512]{1,0:T(8,128)(2,1)S(1)}, bf16[160,512]{1,0:T(8,128)(2,1)S(1)}, u32[]{:S(2)}, u32[]{:S(2)}) collective-permute-start(bf16[160,512]{1,0:T(8,128)(2,1)S(1)} %pre.1.refs_0_), channel_id=1, source_target_pairs={{0,3},{1,0},{2,1},{3,2},{4,7},{5,4},{6,5},{7,6},{8,11},{9,8},{10,9... | collective-permute-start | bytes 491528 | tf_op jit(solution)/shard_map/ppermute | solution.py:377
  81.8 5.4 %collective-permute-done.23.refs_2_ = bf16[64,8192]{1,0:T(8,128)(2,1)S(1)} collective-permute-done((bf16[64,8192]{1,0:T(8,128)(2,1)S(1)}, bf16[64,8192]{1,0:T(8,128)(2,1)S(1)}, u32[]{:S(2)}, u32[]{:S(2)}) %collective-permute-start.23) | collective-permute-done | bytes 1048608 | tf_op jit(solution)/shard_map/ppermute | solution.py:390
  89.6 4.7 %collective-permute-done.16.refs_2_ = bf16[160,512]{1,0:T(8,128)(2,1)S(1)} collective-permute-done((bf16[160,512]{1,0:T(8,128)(2,1)S(1)}, bf16[160,512]{1,0:T(8,128)(2,1)S(1)}, u32[]{:S(2)}, u32[]{:S(2)}) %collective-permute-start.16) | collective-permute-done | bytes 163872 | tf_op jit(solution)/shard_map/ppermute | solution.py:377
  96.1 2.0 %columns.1 = (bf16[128,1280]{1,0:T(8,128)(2,1)S(1)}, bf16[128,1280]{1,0:T(8,128)(2,1)S(1)}, bf16[128,1280]{1,0:T(8,128)(2,1)S(1)}, bf16[128,1280]{1,0:T(8,128)(2,1)S(1)}) custom-call(s32[2]{0:T(128)S(1)} %pad_add_fusion.ids, bf16[160,512]{1,0:T(8,128)(2,1)S(1)} %pre.1.refs_0_, bf16[160,512]{1,0:T(8,128)(2,1)S(1)} %collective-permute-done.15.refs_1_, ...), custom_call_target="tpu_custom_call" | custom-call | flops 939524096 | bytes 2129928 | tf_op jit(solution)/shard_map/columns/pallas_call | solution.py:41
  100.1 7.1 %collective-permute-done.25.refs_3_ = bf16[64,8192]{1,0:T(8,128)(2,1)S(1)} collective-permute-done((bf16[64,8192]{1,0:T(8,128)(2,1)S(1)}, bf16[64,8192]{1,0:T(8,128)(2,1)S(1)}, u32[]{:S(2)}, u32[]{:S(2)}) %collective-permute-start.25) | collective-permute-done | bytes 1048608 | tf_op jit(solution)/shard_map/ppermute | solution.py:390
  107.2 2.9 %collective-permute-start.21 = (bf16[128,1280]{1,0:T(8,128)(2,1)S(1)}, bf16[128,1280]{1,0:T(8,128)(2,1)S(1)}, u32[]{:S(2)}, u32[]{:S(2)}) collective-permute-start(bf16[128,1280]{1,0:T(8,128)(2,1)S(1)} %get-tuple-element.69), channel_id=1, source_target_pairs={{0,1},{1,2},{2,3},{3,0},{4,5},{5,6},{6,7},{7,4},{8,9},{9,10},{10,1... | collective-permute-start | bytes 983048 | tf_op jit(solution)/shard_map/ppermute | solution.py:377
  110.0 2.1 %add.9 = bf16[64,8192]{1,0:T(8,128)(2,1)} custom-call(bf16[64,8192]{1,0:T(8,128)(2,1)S(1)} %get-tuple-element.71.refs_0_, bf16[256,8192]{1,0:T(8,128)(2,1)S(1)} %collective-permute-done.22.refs_1_, bf16[64,8192]{1,0:T(8,128)(2,1)S(1)} %collective-permute-done.24.refs_2_, bf16[64,8192]{1,0:T(8,128)(2,1)S(1)} %collective-permute-done.25.refs_3_), custom_call_target="tpu_custom_call" | custom-call | bytes 5242880 | tf_op jit(solution)/shard_map/add/pallas_call | solution.py:356
  112.8 2.0 %collective-permute-start.27 = (bf16[80,1280]{1,0:T(8,128)(2,1)S(1)}, bf16[80,1280]{1,0:T(8,128)(2,1)S(1)}, u32[]{:S(2)}, u32[]{:S(2)}) collective-permute-start(bf16[80,1280]{1,0:T(8,128)(2,1)S(1)} %get-tuple-element.78), channel_id=1, source_target_pairs={{0,8},{4,20},{8,0},{12,28},{16,24},{20,4},{24,16},{28,12},{1,9},{5... | collective-permute-start | bytes 614408 | tf_op jit(solution)/shard_map/ppermute | solution.py:390
  116.3 13.1 %collective-permute-done.20.refs_2_ = bf16[128,1280]{1,0:T(8,128)(2,1)S(1)} collective-permute-done((bf16[128,1280]{1,0:T(8,128)(2,1)S(1)}, bf16[128,1280]{1,0:T(8,128)(2,1)S(1)}, u32[]{:S(2)}, u32[]{:S(2)}) %collective-permute-start.20) | collective-permute-done | bytes 327712 | tf_op jit(solution)/shard_map/ppermute | solution.py:377
  (68 shorter events, 26.0 us)
Async XLA Ops:
  0.6 17.6 %collective-permute-start = (bf16[64,8192]{1,0:T(8,128)(2,1)}, bf16[64,8192]{1,0:T(8,128)(2,1)S(1)}, u32[]{:S(2)}, u32[]{:S(2)}) collective-permute-start(bf16[64,8192]{1,0:T(8,128)(2,1)} %refs_0_.2), channel_id=1, source_target_pairs={{0,8},{4,20},{8,0},{12,28},{16,24},{20,4},{24,16},{28,12},{1,9},{5... | collective-permute-start | bytes 3145736 | tf_op jit(solution)/shard_map/ppermute | solution.py:390
  8.3 14.6 %collective-permute-start.5 = (bf16[64,8192]{1,0:T(8,128)(2,1)}, bf16[64,8192]{1,0:T(8,128)(2,1)S(1)}, u32[]{:S(2)}, u32[]{:S(2)}) collective-permute-start(bf16[64,8192]{1,0:T(8,128)(2,1)} %refs_0_.2), channel_id=1, source_target_pairs={{0,4},{4,0},{8,12},{12,8},{16,20},{20,16},{24,28},{28,24},{1,5},{5... | collective-permute-start | bytes 3145736 | tf_op jit(solution)/shard_map/ppermute | solution.py:374
  18.3 18.2 %collective-permute-start.1 = (bf16[64,8192]{1,0:T(8,128)(2,1)S(1)}, bf16[64,8192]{1,0:T(8,128)(2,1)S(1)}, u32[]{:S(2)}, u32[]{:S(2)}) collective-permute-start(bf16[64,8192]{1,0:T(8,128)(2,1)S(1)} %copy-done.2), channel_id=1, source_target_pairs={{0,16},{4,12},{8,24},{12,4},{16,0},{20,28},{24,8},{28,20},{1,17},{... | collective-permute-start | bytes 3145736 | tf_op jit(solution)/shard_map/ppermute | solution.py:390
  19.9 24.5 %collective-permute-start.9 = (bf16[64,8192]{1,0:T(8,128)(2,1)S(1)}, bf16[64,8192]{1,0:T(8,128)(2,1)S(1)}, u32[]{:S(2)}, u32[]{:S(2)}) collective-permute-start(bf16[64,8192]{1,0:T(8,128)(2,1)S(1)} %collective-permute-done.refs_1_), channel_id=1, source_target_pairs={{0,16},{4,12},{8,24},{12,4},{16,0},{20,28},{24,8},{28,20},{1,17},{... | collective-permute-start | bytes 3145736 | tf_op jit(solution)/shard_map/ppermute | solution.py:390
  20.4 16.1 %collective-permute-start.7 = (bf16[128,1280]{1,0:T(8,128)(2,1)S(1)}, bf16[128,1280]{1,0:T(8,128)(2,1)S(1)}, u32[]{:S(2)}, u32[]{:S(2)}) collective-permute-start(bf16[128,1280]{1,0:T(8,128)(2,1)S(1)} %get-tuple-element.52), channel_id=1, source_target_pairs={{0,1},{1,2},{2,3},{3,0},{4,5},{5,6},{6,7},{7,4},{8,9},{9,10},{10,1... | collective-permute-start | bytes 983048 | tf_op jit(solution)/shard_map/ppermute | solution.py:377
  22.8 16.0 %collective-permute-start.8 = (bf16[128,1280]{1,0:T(8,128)(2,1)S(1)}, bf16[128,1280]{1,0:T(8,128)(2,1)S(1)}, u32[]{:S(2)}, u32[]{:S(2)}) collective-permute-start(bf16[128,1280]{1,0:T(8,128)(2,1)S(1)} %get-tuple-element.53), channel_id=1, source_target_pairs={{0,3},{1,0},{2,1},{3,2},{4,7},{5,4},{6,5},{7,6},{8,11},{9,8},{10,9... | collective-permute-start | bytes 983048 | tf_op jit(solution)/shard_map/ppermute | solution.py:377
  44.9 26.8 %collective-permute-start.22 = (bf16[256,8192]{1,0:T(8,128)(2,1)S(1)}, bf16[256,8192]{1,0:T(8,128)(2,1)S(1)}, u32[]{:S(2)}, u32[]{:S(2)}) collective-permute-start(bf16[256,8192]{1,0:T(8,128)(2,1)S(1)} %get-tuple-element.51), channel_id=1, source_target_pairs={{0,4},{4,0},{8,12},{12,8},{16,20},{20,16},{24,28},{28,24},{1,5},{5... | collective-permute-start | bytes 12582920 | tf_op jit(solution)/shard_map/ppermute | solution.py:374
  44.9 24.0 %collective-permute-start.18 = (bf16[128,1280]{1,0:T(8,128)(2,1)S(1)}, bf16[128,1280]{1,0:T(8,128)(2,1)S(1)}, u32[]{:S(2)}, u32[]{:S(2)}) collective-permute-start(bf16[128,1280]{1,0:T(8,128)(2,1)S(1)} %get-tuple-element.63), channel_id=1, source_target_pairs={{0,2},{1,3},{2,0},{3,1},{4,6},{5,7},{6,4},{7,5},{8,10},{9,11},{10,... | collective-permute-start | bytes 983048 | tf_op jit(solution)/shard_map/ppermute | solution.py:377
  53.0 15.9 %collective-permute-start.12 = (bf16[128,512]{1,0:T(8,128)(2,1)S(1)}, bf16[128,512]{1,0:T(8,128)(2,1)S(1)}, u32[]{:S(2)}, u32[]{:S(2)}) collective-permute-start(bf16[128,512]{1,0:T(8,128)(2,1)S(1)} %get-tuple-element.60), channel_id=1, source_target_pairs={{0,1},{1,2},{2,3},{3,0},{4,5},{5,6},{6,7},{7,4},{8,9},{9,10},{10,1... | collective-permute-start | bytes 393224 | tf_op jit(solution)/shard_map/ppermute | solution.py:377
  54.0 17.7 %collective-permute-start.13 = (bf16[128,512]{1,0:T(8,128)(2,1)S(1)}, bf16[128,512]{1,0:T(8,128)(2,1)S(1)}, u32[]{:S(2)}, u32[]{:S(2)}) collective-permute-start(bf16[128,512]{1,0:T(8,128)(2,1)S(1)} %get-tuple-element.61), channel_id=1, source_target_pairs={{0,2},{1,3},{2,0},{3,1},{4,6},{5,7},{6,4},{7,5},{8,10},{9,11},{10,... | collective-permute-start | bytes 393224 | tf_op jit(solution)/shard_map/ppermute | solution.py:377
  56.0 15.7 %collective-permute-start.14 = (bf16[128,512]{1,0:T(8,128)(2,1)S(1)}, bf16[128,512]{1,0:T(8,128)(2,1)S(1)}, u32[]{:S(2)}, u32[]{:S(2)}) collective-permute-start(bf16[128,512]{1,0:T(8,128)(2,1)S(1)} %get-tuple-element.62), channel_id=1, source_target_pairs={{0,3},{1,0},{2,1},{3,2},{4,7},{5,4},{6,5},{7,6},{8,11},{9,8},{10,9... | collective-permute-start | bytes 393224 | tf_op jit(solution)/shard_map/ppermute | solution.py:377
  72.3 14.9 %collective-permute-start.23 = (bf16[64,8192]{1,0:T(8,128)(2,1)S(1)}, bf16[64,8192]{1,0:T(8,128)(2,1)S(1)}, u32[]{:S(2)}, u32[]{:S(2)}) collective-permute-start(bf16[64,8192]{1,0:T(8,128)(2,1)S(1)} %add.6), channel_id=1, source_target_pairs={{0,16},{4,12},{8,24},{12,4},{16,0},{20,28},{24,8},{28,20},{1,17},{... | collective-permute-start | bytes 3145736 | tf_op jit(solution)/shard_map/ppermute | solution.py:390
  74.5 15.1 %collective-permute-start.17 = (bf16[160,512]{1,0:T(8,128)(2,1)S(1)}, bf16[160,512]{1,0:T(8,128)(2,1)S(1)}, u32[]{:S(2)}, u32[]{:S(2)}) collective-permute-start(bf16[160,512]{1,0:T(8,128)(2,1)S(1)} %pre.1.refs_0_), channel_id=1, source_target_pairs={{0,3},{1,0},{2,1},{3,2},{4,7},{5,4},{6,5},{7,6},{8,11},{9,8},{10,9... | collective-permute-start | bytes 491528 | tf_op jit(solution)/shard_map/ppermute | solution.py:377
  80.0 14.3 %collective-permute-start.16 = (bf16[160,512]{1,0:T(8,128)(2,1)S(1)}, bf16[160,512]{1,0:T(8,128)(2,1)S(1)}, u32[]{:S(2)}, u32[]{:S(2)}) collective-permute-start(bf16[160,512]{1,0:T(8,128)(2,1)S(1)} %pre.1.refs_0_), channel_id=1, source_target_pairs={{0,2},{1,3},{2,0},{3,1},{4,6},{5,7},{6,4},{7,5},{8,10},{9,11},{10,... | collective-permute-start | bytes 491528 | tf_op jit(solution)/shard_map/ppermute | solution.py:377
  80.0 14.3 %collective-permute-start.15 = (bf16[160,512]{1,0:T(8,128)(2,1)S(1)}, bf16[160,512]{1,0:T(8,128)(2,1)S(1)}, u32[]{:S(2)}, u32[]{:S(2)}) collective-permute-start(bf16[160,512]{1,0:T(8,128)(2,1)S(1)} %pre.1.refs_0_), channel_id=1, source_target_pairs={{0,1},{1,2},{2,3},{3,0},{4,5},{5,6},{6,7},{7,4},{8,9},{9,10},{10,1... | collective-permute-start | bytes 491528 | tf_op jit(solution)/shard_map/ppermute | solution.py:377
  81.2 26.0 %collective-permute-start.25 = (bf16[64,8192]{1,0:T(8,128)(2,1)S(1)}, bf16[64,8192]{1,0:T(8,128)(2,1)S(1)}, u32[]{:S(2)}, u32[]{:S(2)}) collective-permute-start(bf16[64,8192]{1,0:T(8,128)(2,1)S(1)} %add.8), channel_id=1, source_target_pairs={{0,16},{4,12},{8,24},{12,4},{16,0},{20,28},{24,8},{28,20},{1,17},{... | collective-permute-start | bytes 3145736 | tf_op jit(solution)/shard_map/ppermute | solution.py:390
  87.9 22.1 %collective-permute-start.24 = (bf16[64,8192]{1,0:T(8,128)(2,1)S(1)}, bf16[64,8192]{1,0:T(8,128)(2,1)S(1)}, u32[]{:S(2)}, u32[]{:S(2)}) collective-permute-start(bf16[64,8192]{1,0:T(8,128)(2,1)S(1)} %add.7), channel_id=1, source_target_pairs={{0,8},{4,20},{8,0},{12,28},{16,24},{20,4},{24,16},{28,12},{1,9},{5... | collective-permute-start | bytes 3145736 | tf_op jit(solution)/shard_map/ppermute | solution.py:390
  96.0 16.1 %collective-permute-start.26 = (bf16[304,1280]{1,0:T(8,128)(2,1)S(1)}, bf16[304,1280]{1,0:T(8,128)(2,1)S(1)}, u32[]{:S(2)}, u32[]{:S(2)}) collective-permute-start(bf16[304,1280]{1,0:T(8,128)(2,1)S(1)} %get-tuple-element.64), channel_id=1, source_target_pairs={{0,4},{4,0},{8,12},{12,8},{16,20},{20,16},{24,28},{28,24},{1,5},{5... | collective-permute-start | bytes 2334728 | tf_op jit(solution)/shard_map/ppermute | solution.py:374
  98.1 16.7 %collective-permute-start.19 = (bf16[128,1280]{1,0:T(8,128)(2,1)S(1)}, bf16[128,1280]{1,0:T(8,128)(2,1)S(1)}, u32[]{:S(2)}, u32[]{:S(2)}) collective-permute-start(bf16[128,1280]{1,0:T(8,128)(2,1)S(1)} %get-tuple-element.67), channel_id=1, source_target_pairs={{0,3},{1,0},{2,1},{3,2},{4,7},{5,4},{6,5},{7,6},{8,11},{9,8},{10,9... | collective-permute-start | bytes 983048 | tf_op jit(solution)/shard_map/ppermute | solution.py:377
  98.4 31.0 %collective-permute-start.20 = (bf16[128,1280]{1,0:T(8,128)(2,1)S(1)}, bf16[128,1280]{1,0:T(8,128)(2,1)S(1)}, u32[]{:S(2)}, u32[]{:S(2)}) collective-permute-start(bf16[128,1280]{1,0:T(8,128)(2,1)S(1)} %get-tuple-element.68), channel_id=1, source_target_pairs={{0,2},{1,3},{2,0},{3,1},{4,6},{5,7},{6,4},{7,5},{8,10},{9,11},{10,... | collective-permute-start | bytes 983048 | tf_op jit(solution)/shard_map/ppermute | solution.py:377
  107.2 22.3 %collective-permute-start.21 = (bf16[128,1280]{1,0:T(8,128)(2,1)S(1)}, bf16[128,1280]{1,0:T(8,128)(2,1)S(1)}, u32[]{:S(2)}, u32[]{:S(2)}) collective-permute-start(bf16[128,1280]{1,0:T(8,128)(2,1)S(1)} %get-tuple-element.69), channel_id=1, source_target_pairs={{0,1},{1,2},{2,3},{3,0},{4,5},{5,6},{6,7},{7,4},{8,9},{9,10},{10,1... | collective-permute-start | bytes 983048 | tf_op jit(solution)/shard_map/ppermute | solution.py:377
  112.8 16.7 %collective-permute-start.27 = (bf16[80,1280]{1,0:T(8,128)(2,1)S(1)}, bf16[80,1280]{1,0:T(8,128)(2,1)S(1)}, u32[]{:S(2)}, u32[]{:S(2)}) collective-permute-start(bf16[80,1280]{1,0:T(8,128)(2,1)S(1)} %get-tuple-element.78), channel_id=1, source_target_pairs={{0,8},{4,20},{8,0},{12,28},{16,24},{20,4},{24,16},{28,12},{1,9},{5... | collective-permute-start | bytes 614408 | tf_op jit(solution)/shard_map/ppermute | solution.py:390
  114.7 14.7 %collective-permute-start.28 = (bf16[80,1280]{1,0:T(8,128)(2,1)S(1)}, bf16[80,1280]{1,0:T(8,128)(2,1)S(1)}, u32[]{:S(2)}, u32[]{:S(2)}) collective-permute-start(bf16[80,1280]{1,0:T(8,128)(2,1)S(1)} %get-tuple-element.79), channel_id=1, source_target_pairs={{0,16},{4,12},{8,24},{12,4},{16,0},{20,28},{24,8},{28,20},{1,17},{... | collective-permute-start | bytes 614408 | tf_op jit(solution)/shard_map/ppermute | solution.py:390
  114.8 14.6 %collective-permute-start.29 = (bf16[80,1280]{1,0:T(8,128)(2,1)S(1)}, bf16[80,1280]{1,0:T(8,128)(2,1)S(1)}, u32[]{:S(2)}, u32[]{:S(2)}) collective-permute-start(bf16[80,1280]{1,0:T(8,128)(2,1)S(1)} %get-tuple-element.80), channel_id=1, source_target_pairs={{0,24},{4,28},{8,16},{12,20},{16,8},{20,12},{24,0},{28,4},{1,25},{... | collective-permute-start | bytes 614408 | tf_op jit(solution)/shard_map/ppermute | solution.py:390
  (14 other events, 109.5 us)
